TPU v7x, 32 devices: a whole 2x2x4 slice. The times are simulated.
32 devices in a mesh: parts: 2 (over x), wide: 16 (over z, y, core).
Axes of the slice: x: 2, y: 2, z: 4, core: 2. Of those that a mesh axis runs over, the one named last changes fastest.
Arguments:
- inputs: bfloat16 [3, 32768, 128], P(None, ('parts', 'wide')), parts along dimension 1, may hold values from -3 to 3
- state_init: float32 [32768, 128], P(('parts', 'wide')), parts along dimension 0, may hold values from -3 to 3
- cotangent: bfloat16 [3, 32768, 128], P(None, ('parts', 'wide')), parts along dimension 1, may hold values from -1.796875 to 1.796875
- gate_w: bfloat16 [768, 256], replicated, may hold values from -0.21875 to 0.21875
- gate_b: float32 [256], replicated, may hold values from -3 to 3
- cand_w: bfloat16 [768, 128], replicated, may hold values from -0.21875 to 0.21875
- cand_b: float32 [128], replicated, may hold values from -3 to 3
- tile_vals: bfloat16 [256, 4, 128, 128], P(('parts', 'wide')), parts along dimension 0, may hold values from -0.125 to 0.125
- tile_cols: int32 [256, 4], P(('parts', 'wide')), parts along dimension 0, may hold values from 0 to 127, as said below
- tile_counts: int32 [256], P(('parts', 'wide')), parts along dimension 0, may hold values from 3 to 4, as said below
- sector_order: int32 [32768], P(('parts', 'wide')), parts along dimension 0, may hold values from 0 to 1023, as said below
Outputs:
- grad_inputs: bfloat16 [3, 32768, 128], P(None, ('parts', 'wide')), parts along dimension 1
- grad_state_init: float32 [32768, 128], P(('parts', 'wide')), parts along dimension 0
- grad_gate_w: float32 [1536, 256], P('parts'), parts along dimension 0
- grad_gate_b: float32 [512], P('parts'), parts along dimension 0
- grad_cand_w: float32 [1536, 128], P('parts'), parts along dimension 0
- grad_cand_b: float32 [256], P('parts'), parts along dimension 0
There are 2 independent parts, one for each index of `parts`. A program takes and returns all parts, laid end to end along the dimension named above; an argument that names none is the same for every part. Nothing has to cross between parts.
Inputs may be any that keep to these rules, and one draw needn't show every extreme that they name: `tile_cols`: slot 0 of tile row g names g; slots 1 and 2 name g - 1 and g + 1 clipped to 0 and 127; slot 3 names a tile of g // 8 * 8 - 1 to g // 8 * 8 + 8, clipped likewise. `tile_counts`: tile row 0 has 4 live slots and tile row 1 has 3; every row has one of these two counts. `sector_order`: each aligned block of 1024 entries is a permutation of 0 to 1023.
All inputs are finite; a program needn't handle non-finite values.
Results may differ from a plain program's by a relative error of at most 0.007.
Values may be sent and summed in bfloat16 or wider, within the bound.
No kernel may reach another device: no remote copies, remote signals or barrier semaphores. Data moves between devices by JAX's collectives and lax.ppermute only.
A program may use at most 128 MiB of HBM per device.

v0:
```python
import math

import jax
import jax.numpy as jnp
from jax import lax
from jax.sharding import PartitionSpec as P


def padded(block, sides, width):
    for axis, dim in sides:
        count = lax.axis_size(axis)
        forward = [(i, i + 1) for i in range(count - 1)]
        backward = [(target, source) for source, target in forward]
        low = lax.ppermute(
            lax.slice_in_dim(block, block.shape[dim] - width, None, axis=dim), axis, forward
        )
        high = lax.ppermute(lax.slice_in_dim(block, 0, width, axis=dim), axis, backward)
        block = jnp.concatenate([low, block, high], axis=dim)
    return block


def from_behind(block, axis, distance):
    devices = range(lax.axis_size(axis))
    route = [(i - distance, i) for i in devices if i - distance in devices]
    return lax.ppermute(block, axis, route)


def outer_sum(left, right):
    return lax.dot_general(
        left, right, (((0,), (0,)), ((), ())), preferred_element_type=jnp.float32
    )


def diffuse(forward, input_base):
    first_order = forward(input_base).astype(jnp.bfloat16)
    second_order = (2.0 * forward(first_order) - input_base.astype(jnp.float32)).astype(
        jnp.bfloat16
    )
    return (first_order, second_order)


def diffuse_back(backward, grad_zero, grad_one, grad_two):
    through_two = backward(grad_two.astype(jnp.bfloat16))
    grad_one_total = grad_one + 2.0 * through_two
    return grad_zero - grad_two + backward(grad_one_total.astype(jnp.bfloat16))


def make_ops(tile_vals, tile_cols, tile_counts):
    tiles_here = tile_vals.shape[0]
    slot_count = tile_vals.shape[1]
    tile_width = tile_vals.shape[2]
    first_tile = lax.axis_index("wide") * tiles_here - 1
    local_cols = tile_cols - first_tile
    flat_cols = local_cols.reshape(-1)
    live_slots = (jnp.arange(slot_count, dtype=jnp.int32)[None, :] < tile_counts[:, None]).astype(
        jnp.bfloat16
    )
    masked = tile_vals * live_slots[:, :, None, None]

    def forward(row_block):
        feat_count = row_block.shape[1]
        tile_rows = row_block.reshape(tiles_here, tile_width, feat_count)
        extended = padded(tile_rows, (("wide", 0),), 1)
        picked = extended[local_cols]
        product = jnp.einsum("rsab,rsbf->raf", masked, picked, preferred_element_type=jnp.float32)
        return product.reshape(row_block.shape[0], feat_count)

    def backward(grads):
        feat_count = grads.shape[1]
        contrib = jnp.einsum(
            "rsab,raf->rsbf",
            masked,
            grads.reshape(tiles_here, tile_width, feat_count),
            preferred_element_type=jnp.float32,
        )
        extended = (
            jnp.zeros((tiles_here + 2, tile_width, feat_count), jnp.float32)
            .at[flat_cols]
            .add(contrib.reshape(-1, tile_width, feat_count))
        )
        from_upper = from_behind(extended[0], "wide", -1)
        from_lower = from_behind(extended[tiles_here + 1], "wide", 1)
        middle = extended[1 : tiles_here + 1]
        middle = middle.at[tiles_here - 1].add(from_upper)
        middle = middle.at[0].add(from_lower)
        return middle.reshape(grads.shape[0], feat_count)

    return (forward, backward)


def per_device(
    inputs,
    state_init,
    cotangent,
    gate_w,
    gate_b,
    cand_w,
    cand_b,
    tile_vals,
    tile_cols,
    tile_counts,
    sector_order,
):
    forward, backward = make_ops(tile_vals, tile_cols, tile_counts)
    hidden = cand_w.shape[1]
    steps_count = inputs.shape[0]
    row_count = inputs.shape[1]
    ordered_in = inputs[:, sector_order]
    ordered_cot = cotangent[:, sector_order].astype(jnp.float32)
    carried = state_init[sector_order]
    input_terms = [
        (ordered_in[step_index],) + diffuse(forward, ordered_in[step_index])
        for step_index in range(steps_count)
    ]
    saved_steps = []
    for step_index in range(steps_count):
        input_base, input_one, input_two = input_terms[step_index]
        state_b = carried.astype(jnp.bfloat16)
        state_one, state_two = diffuse(forward, state_b)
        gate_feats = jnp.concatenate(
            [input_base, input_one, input_two, state_b, state_one, state_two], axis=1
        )
        gate_pre = jnp.dot(gate_feats, gate_w, preferred_element_type=jnp.float32) + gate_b
        reset_gate = jax.nn.sigmoid(gate_pre[:, :hidden])
        update = jax.nn.sigmoid(gate_pre[:, hidden:])
        reset_state = (reset_gate * carried).astype(jnp.bfloat16)
        reset_one, reset_two = diffuse(forward, reset_state)
        cand_feats = jnp.concatenate(
            [input_base, input_one, input_two, reset_state, reset_one, reset_two], axis=1
        )
        candidate = jnp.tanh(
            jnp.dot(cand_feats, cand_w, preferred_element_type=jnp.float32) + cand_b
        )
        saved_steps.append((carried, gate_feats, cand_feats, reset_gate, update, candidate))
        carried = update * carried + (1.0 - update) * candidate
    grad_state = jnp.zeros((row_count, hidden), jnp.float32)
    total_gw = jnp.zeros(gate_w.shape, jnp.float32)
    total_gb = jnp.zeros(gate_b.shape, jnp.float32)
    total_cw = jnp.zeros(cand_w.shape, jnp.float32)
    total_cb = jnp.zeros(cand_b.shape, jnp.float32)
    input_parts = [None] * steps_count
    for step_index in reversed(range(steps_count)):
        prev_state, gate_feats, cand_feats, reset_gate, update, candidate = saved_steps[step_index]
        grad_state = grad_state + ordered_cot[step_index]
        grad_cand = grad_state * (1.0 - update)
        grad_update = grad_state * (prev_state - candidate)
        grad_prev = grad_state * update
        cand_pre_grad = grad_cand * (1.0 - candidate * candidate)
        cand_pre_b = cand_pre_grad.astype(jnp.bfloat16)
        step_cw = outer_sum(cand_feats, cand_pre_b)
        step_cb = jnp.sum(cand_pre_grad, axis=0)
        cand_feat_grad = jnp.dot(cand_pre_b, cand_w.T, preferred_element_type=jnp.float32)
        reset_grad = diffuse_back(
            backward,
            cand_feat_grad[:, 3 * hidden : 4 * hidden],
            cand_feat_grad[:, 4 * hidden : 5 * hidden],
            cand_feat_grad[:, 5 * hidden :],
        )
        grad_reset = reset_grad * prev_state
        grad_prev = grad_prev + reset_grad * reset_gate
        gate_pre_grad = jnp.concatenate(
            [grad_reset * reset_gate * (1.0 - reset_gate), grad_update * update * (1.0 - update)],
            axis=1,
        )
        gate_pre_b = gate_pre_grad.astype(jnp.bfloat16)
        step_gw = outer_sum(gate_feats, gate_pre_b)
        step_gb = jnp.sum(gate_pre_grad, axis=0)
        gate_feat_grad = jnp.dot(gate_pre_b, gate_w.T, preferred_element_type=jnp.float32)
        grad_prev = grad_prev + diffuse_back(
            backward,
            gate_feat_grad[:, 3 * hidden : 4 * hidden],
            gate_feat_grad[:, 4 * hidden : 5 * hidden],
            gate_feat_grad[:, 5 * hidden :],
        )
        input_parts[step_index] = cand_feat_grad[:, : 3 * hidden] + gate_feat_grad[:, : 3 * hidden]
        total_gw = total_gw + step_gw
        total_gb = total_gb + step_gb
        total_cw = total_cw + step_cw
        total_cb = total_cb + step_cb
        grad_state = grad_prev
    total_gw, total_gb, total_cw, total_cb = lax.psum(
        (total_gw, total_gb, total_cw, total_cb), "wide"
    )
    ordered_grads = jnp.stack(
        [
            diffuse_back(
                backward,
                part_grad[:, :hidden],
                part_grad[:, hidden : 2 * hidden],
                part_grad[:, 2 * hidden :],
            ).astype(jnp.bfloat16)
            for part_grad in input_parts
        ],
        axis=0,
    )
    grad_inputs = (
        jnp.zeros((steps_count, row_count, hidden), jnp.bfloat16)
        .at[:, sector_order]
        .set(ordered_grads)
    )
    grad_state_init = jnp.zeros((row_count, hidden), jnp.float32).at[sector_order].set(grad_state)
    scale = 1.0 / math.sqrt(row_count * lax.axis_size("wide") * steps_count)
    return (
        grad_inputs,
        grad_state_init,
        total_gw * scale,
        total_gb * scale,
        total_cw * scale,
        total_cb * scale,
    )


def solution(mesh):
    return jax.shard_map(
        per_device,
        mesh=mesh,
        in_specs=(
            P(None, ("parts", "wide"), None),
            P(("parts", "wide"), None),
            P(None, ("parts", "wide"), None),
            P(),
            P(),
            P(),
            P(),
            P(("parts", "wide"), None, None, None),
            P(("parts", "wide"), None),
            P(("parts", "wide")),
            P(("parts", "wide")),
        ),
        out_specs=(
            P(None, ("parts", "wide"), None),
            P(("parts", "wide"), None),
            P("parts", None),
            P("parts"),
            P("parts", None),
            P("parts"),
        ),
        check_vma=False,
    )
```

profile of v0, /device:TPU:0, one launch (start us, length us, event | category | flops | bytes accessed | tf_op | source)
XLA Modules:
  0.0 695.1 jit_solution(10739030959837073160)
XLA Ops:
  8.3 4.7 gather_fusion.1
  18.7 5.1 collective-permute-start.8
  59.6 5.1 collective-permute-start.2
  83.2 5.2 collective-permute-start.12
  94.0 5.3 collective-permute-start.14
  107.8 5.2 collective-permute-start.16
  113.0 9.5 %gather_fusion = bf16[1024,3,128]{2,0,1:T(8,128)(2,1)} fusion(bf16[3,1024,128]{2,1,0:T(8,128)(2,1)S(1)} %copy-done.3, s32[1024]{0:T(1024)S(1)} %get-tuple-element.565), kind=kCustom, calls=%fused_computation | custom fusion | bytes 1576960 | tf_op jit(solution)/shard_map/gather | solution.py:109
  129.9 5.2 collective-permute-start.18
  144.7 6.3 collective-permute-start.20
  156.5 5.6 collective-permute-start.22
  171.5 5.5 collective-permute-start.24
  185.2 5.6 collective-permute-start.26
  200.4 6.1 collective-permute-start.28
  213.2 5.6 collective-permute-start.30
  228.3 5.5 collective-permute-start.32
  241.1 5.8 collective-permute-start.34
  261.5 4.7 scatter_fusion
  267.6 5.7 collective-permute-start.37
  276.9 4.7 scatter_fusion.1
  286.0 6.2 collective-permute-start.39
  302.5 4.7 scatter_fusion.14
  311.2 4.7 scatter_fusion.2
  316.0 6.1 collective-permute-start.65
  323.4 5.7 collective-permute-start.41
  336.4 4.7 scatter_fusion.3
  343.1 4.7 scatter_fusion.15
  350.7 6.9 collective-permute-start.67
  357.6 5.3 collective-permute-start.43
  372.1 4.7 scatter_fusion.4
  378.1 5.7 collective-permute-start.45
  392.1 4.7 scatter_fusion.5
  400.5 4.8 collective-permute-start.47
  412.8 4.7 scatter_fusion.12
  421.4 4.7 scatter_fusion.6
  427.4 5.3 collective-permute-start.49
  449.4 4.7 scatter_fusion.7
  456.1 4.7 scatter_fusion.13
  463.6 6.4 collective-permute-start.63
  482.9 4.7 scatter_fusion.8
  508.8 5.5 collective-permute-start.55
  532.7 4.7 scatter_fusion.17
  540.3 6.0 collective-permute-start.57
  552.4 36.1 %all-reduce = (f32[256]{0:T(256)S(1)}, f32[128]{0:T(128)}) all-reduce(f32[256]{0:T(256)} %add_add_fusion, f32[128]{0:T(128)} %add_add_fusion.1), channel_id=1, replica_groups=mesh['parts'=2,'wide'=16] {'wide'}, use_global_device_ids=true, to_apply=%region_24.0 | all-reduce | flops 384 | bytes 3072 | tf_op jit(solution)/shard_map/psum | solution.py:181
  600.9 4.7 scatter_fusion.11
  613.8 4.7 scatter_fusion.18
  629.9 26.6 %scatter_fusion.16 = bf16[3,1024,128]{2,0,1:T(4,128)(2,1)S(1)} fusion(bf16[3,1024,128]{2,0,1:T(4,128)(2,1)S(1)} %broadcast_in_dim.8, s32[1024]{0:T(1024)S(1)} %get-tuple-element.566, bf16[1024,3,128]{2,1,0:T(4,128)(2,1)S(1)} %copy.57), kind=kCustom, calls=%fused_computation.37 | custom fusion | bytes 2363392 | tf_op jit(solution)/shard_map/scatter | solution.py:199
  658.0 4.8 scatter_custom_fusion.19
  662.8 22.1 %all-reduce.4.cloned.1.call-done = (f32[768,256]{1,0:T(8,128)}, f32[768,128]{1,0:T(8,128)}) async-done(((f32[768,256]{1,0:T(8,128)}, f32[768,128]{1,0:T(8,128)}), (f32[768,256]{1,0:T(8,128)}, f32[768,128]{1,0:T(8,128)})) %all-reduce.4.cloned.1.call-update) | async-done | bytes 1179664 | tf_op jit(solution)/shard_map/psum | solution.py:181
  (609 shorter events, 353.0 us)
Async XLA Ops:
  7.2 677.7 %all-reduce.4.cloned.1.call-start = ((), (), s32[]{:S(2)}) async-start(), calls=%async_computation | async-start | bytes 2359296 | tf_op jit(solution)/shard_map/psum | solution.py:181
  13.0 17.7 %collective-permute-start.1 = (bf16[1,128,128]{2,1,0:T(8,128)(2,1)S(1)}, bf16[1,128,128]{2,1,0:T(8,128)(2,1)S(1)}, u32[]{:S(2)}, u32[]{:S(2)}) collective-permute-start(bf16[1,128,128]{2,1,0:T(8,128)(2,1)S(1)} %get-tuple-element.490), channel_id=1, source_target_pairs={{1,0},{2,1},{3,2},{4,3},{5,4},{6,5},{7,6},{8,7},{9,8},{10,9},{11,1... | collective-permute-start | bytes 98312 | tf_op jit(solution)/shard_map/ppermute | solution.py:17
  14.3 20.7 %collective-permute-start = (bf16[1,128,128]{2,1,0:T(8,128)(2,1)S(1)}, bf16[1,128,128]{2,1,0:T(8,128)(2,1)S(1)}, u32[]{:S(2)}, u32[]{:S(2)}) collective-permute-start(bf16[1,128,128]{2,1,0:T(8,128)(2,1)S(1)} %get-tuple-element.491), channel_id=1, source_target_pairs={{0,1},{1,2},{2,3},{3,4},{4,5},{5,6},{6,7},{7,8},{8,9},{9,10},{10,1... | collective-permute-start | bytes 98312 | tf_op jit(solution)/shard_map/ppermute | solution.py:14
  17.4 19.4 %collective-permute-start.9 = (bf16[1,128,128]{2,1,0:T(8,128)(2,1)S(1)}, bf16[1,128,128]{2,1,0:T(8,128)(2,1)S(1)}, u32[]{:S(2)}, u32[]{:S(2)}) collective-permute-start(bf16[1,128,128]{2,1,0:T(8,128)(2,1)S(1)} %get-tuple-element.492), channel_id=1, source_target_pairs={{1,0},{2,1},{3,2},{4,3},{5,4},{6,5},{7,6},{8,7},{9,8},{10,9},{11,1... | collective-permute-start | bytes 98312 | tf_op jit(solution)/shard_map/ppermute | solution.py:17
  18.7 18.1 %collective-permute-start.8 = (bf16[1,128,128]{2,1,0:T(8,128)(2,1)S(1)}, bf16[1,128,128]{2,1,0:T(8,128)(2,1)S(1)}, u32[]{:S(2)}, u32[]{:S(2)}) collective-permute-start(bf16[1,128,128]{2,1,0:T(8,128)(2,1)S(1)} %get-tuple-element.487), channel_id=1, source_target_pairs={{0,1},{1,2},{2,3},{3,4},{4,5},{5,6},{6,7},{7,8},{8,9},{9,10},{10,1... | collective-permute-start | bytes 98312 | tf_op jit(solution)/shard_map/ppermute | solution.py:14
  23.8 22.6 %collective-permute-start.5 = (bf16[1,128,128]{2,1,0:T(8,128)(2,1)S(1)}, bf16[1,128,128]{2,1,0:T(8,128)(2,1)S(1)}, u32[]{:S(2)}, u32[]{:S(2)}) collective-permute-start(bf16[1,128,128]{2,1,0:T(8,128)(2,1)S(1)} %get-tuple-element.488), channel_id=1, source_target_pairs={{1,0},{2,1},{3,2},{4,3},{5,4},{6,5},{7,6},{8,7},{9,8},{10,9},{11,1... | collective-permute-start | bytes 98312 | tf_op jit(solution)/shard_map/ppermute | solution.py:17
  30.8 15.7 %collective-permute-start.4 = (bf16[1,128,128]{2,1,0:T(8,128)(2,1)S(1)}, bf16[1,128,128]{2,1,0:T(8,128)(2,1)S(1)}, u32[]{:S(2)}, u32[]{:S(2)}) collective-permute-start(bf16[1,128,128]{2,1,0:T(8,128)(2,1)S(1)} %get-tuple-element.489), channel_id=1, source_target_pairs={{0,1},{1,2},{2,3},{3,4},{4,5},{5,6},{6,7},{7,8},{8,9},{9,10},{10,1... | collective-permute-start | bytes 98312 | tf_op jit(solution)/shard_map/ppermute | solution.py:14
  40.8 18.7 %collective-permute-start.11 = (bf16[1,128,128]{2,1,0:T(8,128)(2,1)S(1)}, bf16[1,128,128]{2,1,0:T(8,128)(2,1)S(1)}, u32[]{:S(2)}, u32[]{:S(2)}) collective-permute-start(bf16[1,128,128]{2,1,0:T(8,128)(2,1)S(1)} %get-tuple-element.560), channel_id=1, source_target_pairs={{1,0},{2,1},{3,2},{4,3},{5,4},{6,5},{7,6},{8,7},{9,8},{10,9},{11,1... | collective-permute-start | bytes 98312 | tf_op jit(solution)/shard_map/ppermute | solution.py:17
  42.1 22.5 %collective-permute-start.10 = (bf16[1,128,128]{2,1,0:T(8,128)(2,1)S(1)}, bf16[1,128,128]{2,1,0:T(8,128)(2,1)S(1)}, u32[]{:S(2)}, u32[]{:S(2)}) collective-permute-start(bf16[1,128,128]{2,1,0:T(8,128)(2,1)S(1)} %get-tuple-element.559), channel_id=1, source_target_pairs={{0,1},{1,2},{2,3},{3,4},{4,5},{5,6},{6,7},{7,8},{8,9},{9,10},{10,1... | collective-permute-start | bytes 98312 | tf_op jit(solution)/shard_map/ppermute | solution.py:14
  50.6 18.3 %collective-permute-start.7 = (bf16[1,128,128]{2,1,0:T(8,128)(2,1)}, bf16[1,128,128]{2,1,0:T(8,128)(2,1)S(1)}, u32[]{:S(2)}, u32[]{:S(2)}) collective-permute-start(bf16[1,128,128]{2,1,0:T(8,128)(2,1)} %get-tuple-element.562), channel_id=1, source_target_pairs={{1,0},{2,1},{3,2},{4,3},{5,4},{6,5},{7,6},{8,7},{9,8},{10,9},{11,1... | collective-permute-start | bytes 98312 | tf_op jit(solution)/shard_map/ppermute | solution.py:17
  51.9 17.1 %collective-permute-start.6 = (bf16[1,128,128]{2,1,0:T(8,128)(2,1)}, bf16[1,128,128]{2,1,0:T(8,128)(2,1)S(1)}, u32[]{:S(2)}, u32[]{:S(2)}) collective-permute-start(bf16[1,128,128]{2,1,0:T(8,128)(2,1)} %get-tuple-element.561), channel_id=1, source_target_pairs={{0,1},{1,2},{2,3},{3,4},{4,5},{5,6},{6,7},{7,8},{8,9},{9,10},{10,1... | collective-permute-start | bytes 98312 | tf_op jit(solution)/shard_map/ppermute | solution.py:14
  56.8 16.4 %collective-permute-start.3 = (bf16[1,128,128]{2,1,0:T(8,128)(2,1)}, bf16[1,128,128]{2,1,0:T(8,128)(2,1)S(1)}, u32[]{:S(2)}, u32[]{:S(2)}) collective-permute-start(bf16[1,128,128]{2,1,0:T(8,128)(2,1)} %get-tuple-element.564), channel_id=1, source_target_pairs={{1,0},{2,1},{3,2},{4,3},{5,4},{6,5},{7,6},{8,7},{9,8},{10,9},{11,1... | collective-permute-start | bytes 98312 | tf_op jit(solution)/shard_map/ppermute | solution.py:17
  59.6 13.6 %collective-permute-start.2 = (bf16[1,128,128]{2,1,0:T(8,128)(2,1)S(1)}, bf16[1,128,128]{2,1,0:T(8,128)(2,1)S(1)}, u32[]{:S(2)}, u32[]{:S(2)}) collective-permute-start(bf16[1,128,128]{2,1,0:T(8,128)(2,1)S(1)} %get-tuple-element.563), channel_id=1, source_target_pairs={{0,1},{1,2},{2,3},{3,4},{4,5},{5,6},{6,7},{7,8},{8,9},{9,10},{10,1... | collective-permute-start | bytes 98312 | tf_op jit(solution)/shard_map/ppermute | solution.py:14
  106.5 18.6 %collective-permute-start.17 = (bf16[1,128,128]{2,1,0:T(8,128)(2,1)}, bf16[1,128,128]{2,1,0:T(8,128)(2,1)S(1)}, u32[]{:S(2)}, u32[]{:S(2)}) collective-permute-start(bf16[1,128,128]{2,1,0:T(8,128)(2,1)} %get-tuple-element.554), channel_id=1, source_target_pairs={{1,0},{2,1},{3,2},{4,3},{5,4},{6,5},{7,6},{8,7},{9,8},{10,9},{11,1... | collective-permute-start | bytes 98312 | tf_op jit(solution)/shard_map/ppermute | solution.py:17
  107.8 17.3 %collective-permute-start.16 = (bf16[1,128,128]{2,1,0:T(8,128)(2,1)S(1)}, bf16[1,128,128]{2,1,0:T(8,128)(2,1)S(1)}, u32[]{:S(2)}, u32[]{:S(2)}) collective-permute-start(bf16[1,128,128]{2,1,0:T(8,128)(2,1)S(1)} %get-tuple-element.553), channel_id=1, source_target_pairs={{0,1},{1,2},{2,3},{3,4},{4,5},{5,6},{6,7},{7,8},{8,9},{9,10},{10,1... | collective-permute-start | bytes 98312 | tf_op jit(solution)/shard_map/ppermute | solution.py:14
  143.4 8.4 %collective-permute-start.21 = (bf16[1,128,128]{2,1,0:T(8,128)(2,1)S(1)}, bf16[1,128,128]{2,1,0:T(8,128)(2,1)S(1)}, u32[]{:S(2)}, u32[]{:S(2)}) collective-permute-start(bf16[1,128,128]{2,1,0:T(8,128)(2,1)S(1)} %get-tuple-element.550), channel_id=1, source_target_pairs={{1,0},{2,1},{3,2},{4,3},{5,4},{6,5},{7,6},{8,7},{9,8},{10,9},{11,1... | collective-permute-start | bytes 98312 | tf_op jit(solution)/shard_map/ppermute | solution.py:17
  155.2 7.7 %collective-permute-start.23 = (bf16[1,128,128]{2,1,0:T(8,128)(2,1)S(1)}, bf16[1,128,128]{2,1,0:T(8,128)(2,1)S(1)}, u32[]{:S(2)}, u32[]{:S(2)}) collective-permute-start(bf16[1,128,128]{2,1,0:T(8,128)(2,1)S(1)} %get-tuple-element.548), channel_id=1, source_target_pairs={{1,0},{2,1},{3,2},{4,3},{5,4},{6,5},{7,6},{8,7},{9,8},{10,9},{11,1... | collective-permute-start | bytes 98312 | tf_op jit(solution)/shard_map/ppermute | solution.py:17
  170.2 10.3 %collective-permute-start.25 = (bf16[1,128,128]{2,1,0:T(8,128)(2,1)S(1)}, bf16[1,128,128]{2,1,0:T(8,128)(2,1)S(1)}, u32[]{:S(2)}, u32[]{:S(2)}) collective-permute-start(bf16[1,128,128]{2,1,0:T(8,128)(2,1)S(1)} %get-tuple-element.546), channel_id=1, source_target_pairs={{1,0},{2,1},{3,2},{4,3},{5,4},{6,5},{7,6},{8,7},{9,8},{10,9},{11,1... | collective-permute-start | bytes 98312 | tf_op jit(solution)/shard_map/ppermute | solution.py:17
  171.5 9.0 %collective-permute-start.24 = (bf16[1,128,128]{2,1,0:T(8,128)(2,1)S(1)}, bf16[1,128,128]{2,1,0:T(8,128)(2,1)S(1)}, u32[]{:S(2)}, u32[]{:S(2)}) collective-permute-start(bf16[1,128,128]{2,1,0:T(8,128)(2,1)S(1)} %get-tuple-element.545), channel_id=1, source_target_pairs={{0,1},{1,2},{2,3},{3,4},{4,5},{5,6},{6,7},{7,8},{8,9},{9,10},{10,1... | collective-permute-start | bytes 98312 | tf_op jit(solution)/shard_map/ppermute | solution.py:14
  183.9 7.7 %collective-permute-start.27 = (bf16[1,128,128]{2,1,0:T(8,128)(2,1)S(1)}, bf16[1,128,128]{2,1,0:T(8,128)(2,1)S(1)}, u32[]{:S(2)}, u32[]{:S(2)}) collective-permute-start(bf16[1,128,128]{2,1,0:T(8,128)(2,1)S(1)} %get-tuple-element.544), channel_id=1, source_target_pairs={{1,0},{2,1},{3,2},{4,3},{5,4},{6,5},{7,6},{8,7},{9,8},{10,9},{11,1... | collective-permute-start | bytes 98312 | tf_op jit(solution)/shard_map/ppermute | solution.py:17
  199.1 9.3 %collective-permute-start.29 = (bf16[1,128,128]{2,1,0:T(8,128)(2,1)S(1)}, bf16[1,128,128]{2,1,0:T(8,128)(2,1)S(1)}, u32[]{:S(2)}, u32[]{:S(2)}) collective-permute-start(bf16[1,128,128]{2,1,0:T(8,128)(2,1)S(1)} %get-tuple-element.542), channel_id=1, source_target_pairs={{1,0},{2,1},{3,2},{4,3},{5,4},{6,5},{7,6},{8,7},{9,8},{10,9},{11,1... | collective-permute-start | bytes 98312 | tf_op jit(solution)/shard_map/ppermute | solution.py:17
  200.4 8.0 %collective-permute-start.28 = (bf16[1,128,128]{2,1,0:T(8,128)(2,1)S(1)}, bf16[1,128,128]{2,1,0:T(8,128)(2,1)S(1)}, u32[]{:S(2)}, u32[]{:S(2)}) collective-permute-start(bf16[1,128,128]{2,1,0:T(8,128)(2,1)S(1)} %get-tuple-element.541), channel_id=1, source_target_pairs={{0,1},{1,2},{2,3},{3,4},{4,5},{5,6},{6,7},{7,8},{8,9},{9,10},{10,1... | collective-permute-start | bytes 98312 | tf_op jit(solution)/shard_map/ppermute | solution.py:14
  239.8 7.8 %collective-permute-start.35 = (bf16[1,128,128]{2,1,0:T(8,128)(2,1)S(1)}, bf16[1,128,128]{2,1,0:T(8,128)(2,1)S(1)}, u32[]{:S(2)}, u32[]{:S(2)}) collective-permute-start(bf16[1,128,128]{2,1,0:T(8,128)(2,1)S(1)} %get-tuple-element.536), channel_id=1, source_target_pairs={{1,0},{2,1},{3,2},{4,3},{5,4},{6,5},{7,6},{8,7},{9,8},{10,9},{11,1... | collective-permute-start | bytes 98312 | tf_op jit(solution)/shard_map/ppermute | solution.py:17
  281.7 10.6 %collective-permute-start.38 = (f32[128,128]{1,0:T(8,128)S(1)}, f32[128,128]{1,0:T(8,128)S(1)}, u32[]{:S(2)}, u32[]{:S(2)}) collective-permute-start(f32[128,128]{1,0:T(8,128)S(1)} %get-tuple-element.532), channel_id=1, source_target_pairs={{1,0},{2,1},{3,2},{4,3},{5,4},{6,5},{7,6},{8,7},{9,8},{10,9},{11,1... | collective-permute-start | bytes 196616 | tf_op jit(solution)/shard_map/ppermute | solution.py:25
  307.9 21.4 %collective-permute-start.64 = (f32[128,128]{1,0:T(8,128)}, f32[128,128]{1,0:T(8,128)}, u32[]{:S(2)}, u32[]{:S(2)}) collective-permute-start(f32[128,128]{1,0:T(8,128)} %get-tuple-element.530), channel_id=1, source_target_pairs={{1,0},{2,1},{3,2},{4,3},{5,4},{6,5},{7,6},{8,7},{9,8},{10,9},{11,1... | collective-permute-start | bytes 196616 | tf_op jit(solution)/shard_map/ppermute | solution.py:25
  316.0 14.2 %collective-permute-start.65 = (f32[128,128]{1,0:T(8,128)}, f32[128,128]{1,0:T(8,128)S(1)}, u32[]{:S(2)}, u32[]{:S(2)}) collective-permute-start(f32[128,128]{1,0:T(8,128)} %get-tuple-element.529), channel_id=1, source_target_pairs={{0,1},{1,2},{2,3},{3,4},{4,5},{5,6},{6,7},{7,8},{8,9},{9,10},{10,1... | collective-permute-start | bytes 196616 | tf_op jit(solution)/shard_map/ppermute | solution.py:25
  322.1 11.2 %collective-permute-start.40 = (f32[128,128]{1,0:T(8,128)S(1)}, f32[128,128]{1,0:T(8,128)S(1)}, u32[]{:S(2)}, u32[]{:S(2)}) collective-permute-start(f32[128,128]{1,0:T(8,128)S(1)} %get-tuple-element.526), channel_id=1, source_target_pairs={{1,0},{2,1},{3,2},{4,3},{5,4},{6,5},{7,6},{8,7},{9,8},{10,9},{11,1... | collective-permute-start | bytes 196616 | tf_op jit(solution)/shard_map/ppermute | solution.py:25
  323.4 9.9 %collective-permute-start.41 = (f32[128,128]{1,0:T(8,128)S(1)}, f32[128,128]{1,0:T(8,128)S(1)}, u32[]{:S(2)}, u32[]{:S(2)}) collective-permute-start(f32[128,128]{1,0:T(8,128)S(1)} %get-tuple-element.525), channel_id=1, source_target_pairs={{0,1},{1,2},{2,3},{3,4},{4,5},{5,6},{6,7},{7,8},{8,9},{9,10},{10,1... | collective-permute-start | bytes 196616 | tf_op jit(solution)/shard_map/ppermute | solution.py:25
  341.8 21.1 %collective-permute-start.42 = (f32[128,128]{1,0:T(8,128)}, f32[128,128]{1,0:T(8,128)}, u32[]{:S(2)}, u32[]{:S(2)}) collective-permute-start(f32[128,128]{1,0:T(8,128)} %get-tuple-element.524), channel_id=1, source_target_pairs={{1,0},{2,1},{3,2},{4,3},{5,4},{6,5},{7,6},{8,7},{9,8},{10,9},{11,1... | collective-permute-start | bytes 196616 | tf_op jit(solution)/shard_map/ppermute | solution.py:25
  349.4 37.3 %collective-permute-start.66 = (f32[128,128]{1,0:T(8,128)}, f32[128,128]{1,0:T(8,128)S(1)}, u32[]{:S(2)}, u32[]{:S(2)}) collective-permute-start(f32[128,128]{1,0:T(8,128)} %get-tuple-element.528), channel_id=1, source_target_pairs={{1,0},{2,1},{3,2},{4,3},{5,4},{6,5},{7,6},{8,7},{9,8},{10,9},{11,1... | collective-permute-start | bytes 196616 | tf_op jit(solution)/shard_map/ppermute | solution.py:25
  350.7 36.7 %collective-permute-start.67 = (f32[128,128]{1,0:T(8,128)}, f32[128,128]{1,0:T(8,128)S(1)}, u32[]{:S(2)}, u32[]{:S(2)}) collective-permute-start(f32[128,128]{1,0:T(8,128)} %get-tuple-element.527), channel_id=1, source_target_pairs={{0,1},{1,2},{2,3},{3,4},{4,5},{5,6},{6,7},{7,8},{8,9},{9,10},{10,1... | collective-permute-start | bytes 196616 | tf_op jit(solution)/shard_map/ppermute | solution.py:25
  376.8 12.1 %collective-permute-start.44 = (f32[128,128]{1,0:T(8,128)S(1)}, f32[128,128]{1,0:T(8,128)S(1)}, u32[]{:S(2)}, u32[]{:S(2)}) collective-permute-start(f32[128,128]{1,0:T(8,128)S(1)} %get-tuple-element.522), channel_id=1, source_target_pairs={{1,0},{2,1},{3,2},{4,3},{5,4},{6,5},{7,6},{8,7},{9,8},{10,9},{11,1... | collective-permute-start | bytes 196616 | tf_op jit(solution)/shard_map/ppermute | solution.py:25
  378.1 10.8 %collective-permute-start.45 = (f32[128,128]{1,0:T(8,128)S(1)}, f32[128,128]{1,0:T(8,128)S(1)}, u32[]{:S(2)}, u32[]{:S(2)}) collective-permute-start(f32[128,128]{1,0:T(8,128)S(1)} %get-tuple-element.521), channel_id=1, source_target_pairs={{0,1},{1,2},{2,3},{3,4},{4,5},{5,6},{6,7},{7,8},{8,9},{9,10},{10,1... | collective-permute-start | bytes 196616 | tf_op jit(solution)/shard_map/ppermute | solution.py:25
  396.8 8.6 %collective-permute-start.46 = (f32[128,128]{1,0:T(8,128)S(1)}, f32[128,128]{1,0:T(8,128)S(1)}, u32[]{:S(2)}, u32[]{:S(2)}) collective-permute-start(f32[128,128]{1,0:T(8,128)S(1)} %get-tuple-element.520), channel_id=1, source_target_pairs={{1,0},{2,1},{3,2},{4,3},{5,4},{6,5},{7,6},{8,7},{9,8},{10,9},{11,1... | collective-permute-start | bytes 196616 | tf_op jit(solution)/shard_map/ppermute | solution.py:25
  418.1 24.1 %collective-permute-start.60 = (f32[128,128]{1,0:T(8,128)}, f32[128,128]{1,0:T(8,128)}, u32[]{:S(2)}, u32[]{:S(2)}) collective-permute-start(f32[128,128]{1,0:T(8,128)} %get-tuple-element.518), channel_id=1, source_target_pairs={{1,0},{2,1},{3,2},{4,3},{5,4},{6,5},{7,6},{8,7},{9,8},{10,9},{11,1... | collective-permute-start | bytes 196616 | tf_op jit(solution)/shard_map/ppermute | solution.py:25
  426.1 20.1 %collective-permute-start.48 = (f32[128,128]{1,0:T(8,128)S(1)}, f32[128,128]{1,0:T(8,128)S(1)}, u32[]{:S(2)}, u32[]{:S(2)}) collective-permute-start(f32[128,128]{1,0:T(8,128)S(1)} %get-tuple-element.514), channel_id=1, source_target_pairs={{1,0},{2,1},{3,2},{4,3},{5,4},{6,5},{7,6},{8,7},{9,8},{10,9},{11,1... | collective-permute-start | bytes 196616 | tf_op jit(solution)/shard_map/ppermute | solution.py:25
  427.4 18.8 %collective-permute-start.49 = (f32[128,128]{1,0:T(8,128)S(1)}, f32[128,128]{1,0:T(8,128)S(1)}, u32[]{:S(2)}, u32[]{:S(2)}) collective-permute-start(f32[128,128]{1,0:T(8,128)S(1)} %get-tuple-element.513), channel_id=1, source_target_pairs={{0,1},{1,2},{2,3},{3,4},{4,5},{5,6},{6,7},{7,8},{8,9},{9,10},{10,1... | collective-permute-start | bytes 196616 | tf_op jit(solution)/shard_map/ppermute | solution.py:25
  454.7 19.8 %collective-permute-start.50 = (f32[128,128]{1,0:T(8,128)}, f32[128,128]{1,0:T(8,128)S(1)}, u32[]{:S(2)}, u32[]{:S(2)}) collective-permute-start(f32[128,128]{1,0:T(8,128)} %get-tuple-element.512), channel_id=1, source_target_pairs={{1,0},{2,1},{3,2},{4,3},{5,4},{6,5},{7,6},{8,7},{9,8},{10,9},{11,1... | collective-permute-start | bytes 196616 | tf_op jit(solution)/shard_map/ppermute | solution.py:25
  462.3 29.6 %collective-permute-start.62 = (f32[128,128]{1,0:T(8,128)}, f32[128,128]{1,0:T(8,128)}, u32[]{:S(2)}, u32[]{:S(2)}) collective-permute-start(f32[128,128]{1,0:T(8,128)} %get-tuple-element.516), channel_id=1, source_target_pairs={{1,0},{2,1},{3,2},{4,3},{5,4},{6,5},{7,6},{8,7},{9,8},{10,9},{11,1... | collective-permute-start | bytes 196616 | tf_op jit(solution)/shard_map/ppermute | solution.py:25
  463.6 29.1 %collective-permute-start.63 = (f32[128,128]{1,0:T(8,128)}, f32[128,128]{1,0:T(8,128)}, u32[]{:S(2)}, u32[]{:S(2)}) collective-permute-start(f32[128,128]{1,0:T(8,128)} %get-tuple-element.515), channel_id=1, source_target_pairs={{0,1},{1,2},{2,3},{3,4},{4,5},{5,6},{6,7},{7,8},{8,9},{9,10},{10,1... | collective-permute-start | bytes 196616 | tf_op jit(solution)/shard_map/ppermute | solution.py:25
  487.6 10.3 %collective-permute-start.52 = (f32[128,128]{1,0:T(8,128)S(1)}, f32[128,128]{1,0:T(8,128)S(1)}, u32[]{:S(2)}, u32[]{:S(2)}) collective-permute-start(f32[128,128]{1,0:T(8,128)S(1)} %get-tuple-element.510), channel_id=1, source_target_pairs={{1,0},{2,1},{3,2},{4,3},{5,4},{6,5},{7,6},{8,7},{9,8},{10,9},{11,1... | collective-permute-start | bytes 196616 | tf_op jit(solution)/shard_map/ppermute | solution.py:25
  539.0 54.7 %collective-permute-start.56 = (f32[128,128]{1,0:T(8,128)}, f32[128,128]{1,0:T(8,128)}, u32[]{:S(2)}, u32[]{:S(2)}) collective-permute-start(f32[128,128]{1,0:T(8,128)} %get-tuple-element.506), channel_id=1, source_target_pairs={{1,0},{2,1},{3,2},{4,3},{5,4},{6,5},{7,6},{8,7},{9,8},{10,9},{11,1... | collective-permute-start | bytes 196616 | tf_op jit(solution)/shard_map/ppermute | solution.py:25
  540.3 54.9 %collective-permute-start.57 = (f32[128,128]{1,0:T(8,128)}, f32[128,128]{1,0:T(8,128)}, u32[]{:S(2)}, u32[]{:S(2)}) collective-permute-start(f32[128,128]{1,0:T(8,128)} %get-tuple-element.505), channel_id=1, source_target_pairs={{0,1},{1,2},{2,3},{3,4},{4,5},{5,6},{6,7},{7,8},{8,9},{9,10},{10,1... | collective-permute-start | bytes 196616 | tf_op jit(solution)/shard_map/ppermute | solution.py:25
  546.3 61.3 %collective-permute-start.68 = (f32[128,128]{1,0:T(8,128)}, f32[128,128]{1,0:T(8,128)S(1)}, u32[]{:S(2)}, u32[]{:S(2)}) collective-permute-start(f32[128,128]{1,0:T(8,128)} %get-tuple-element.502), channel_id=1, source_target_pairs={{1,0},{2,1},{3,2},{4,3},{5,4},{6,5},{7,6},{8,7},{9,8},{10,9},{11,1... | collective-permute-start | bytes 196616 | tf_op jit(solution)/shard_map/ppermute | solution.py:25
  547.6 60.6 %collective-permute-start.69 = (f32[128,128]{1,0:T(8,128)}, f32[128,128]{1,0:T(8,128)S(1)}, u32[]{:S(2)}, u32[]{:S(2)}) collective-permute-start(f32[128,128]{1,0:T(8,128)} %get-tuple-element.501), channel_id=1, source_target_pairs={{0,1},{1,2},{2,3},{3,4},{4,5},{5,6},{6,7},{7,8},{8,9},{9,10},{10,1... | collective-permute-start | bytes 196616 | tf_op jit(solution)/shard_map/ppermute | solution.py:25
  606.2 20.8 %collective-permute-start.58 = (f32[128,128]{1,0:T(8,128)}, f32[128,128]{1,0:T(8,128)}, u32[]{:S(2)}, u32[]{:S(2)}) collective-permute-start(f32[128,128]{1,0:T(8,128)} %get-tuple-element.504), channel_id=1, source_target_pairs={{1,0},{2,1},{3,2},{4,3},{5,4},{6,5},{7,6},{8,7},{9,8},{10,9},{11,1... | collective-permute-start | bytes 196616 | tf_op jit(solution)/shard_map/ppermute | solution.py:25
  619.4 8.5 %collective-permute-start.59 = (f32[128,128]{1,0:T(8,128)S(1)}, f32[128,128]{1,0:T(8,128)S(1)}, u32[]{:S(2)}, u32[]{:S(2)}) collective-permute-start(f32[128,128]{1,0:T(8,128)S(1)} %copy-done.87), channel_id=1, source_target_pairs={{0,1},{1,2},{2,3},{3,4},{4,5},{5,6},{6,7},{7,8},{8,9},{9,10},{10,1... | collective-permute-start | bytes 196616 | tf_op jit(solution)/shard_map/ppermute | solution.py:25
  623.7 33.8 %collective-permute-start.71 = (f32[128,128]{1,0:T(8,128)S(1)}, f32[128,128]{1,0:T(8,128)S(1)}, u32[]{:S(2)}, u32[]{:S(2)}) collective-permute-start(f32[128,128]{1,0:T(8,128)S(1)} %get-tuple-element.499), channel_id=1, source_target_pairs={{0,1},{1,2},{2,3},{3,4},{4,5},{5,6},{6,7},{7,8},{8,9},{9,10},{10,1... | collective-permute-start | bytes 196616 | tf_op jit(solution)/shard_map/ppermute | solution.py:25
  (126 other events, 915.9 us)
Sparse Core Ops, SparseCore 0:
  593.8 90.9 all-reduce.3
where the time goes:
time: 709 us; the launch traced here: 695 us
  starting transfers between devices  233 us (33%)
  other arithmetic  151 us (21%)
  local copies, waits for them, and re-layouts  125 us (18%)
  matrix products  103 us (15%)
  blocking collectives  36.1 us (5%)
  waiting for transfers between devices  29.1 us (4%)
  between operations  17.4 us (2%)
    ppermute x36, starting transfers between devices, from_behind(): return lax.ppermute(block, axis, route)  117 us
    ppermute x18, starting transfers between devices, padded(): lax.ppermute(lax.slice_in_dim(block, block.shape[dim] - width, None, axis...  92.8 us
    scatter-add x18, other arithmetic, backward(): extended = jnp.zeros((tiles_here + 2, tile_width, feat_count), jnp.float3...  83.9 us
    psum x1, blocking collectives, per_device(): lax.psum((total_gw, total_gb, total_cw, total_cb), 'wide')  36.1 us
    dot_general x18, matrix products, backward(): jnp.einsum('rsab,raf->rsbf', masked, grads.reshape(tiles_here, tile_width...  34.9 us
    unnamed x218, local copies, waits for them, and re-layouts  34.5 us
    gather x18, local copies, waits for them, and re-layouts, forward(): picked = extended[local_cols]  30.8 us
    dot_general x18, matrix products, forward(): jnp.einsum('rsab,rsbf->raf', masked, picked, preferred_element_type=jnp.f...  30.3 us
  transfers between devices with their start and end apart: 73, of which 15 were waited for; matrix products, arithmetic and copies ran while one was open for 27% of the time, Pallas kernels for 0%

commit v1 on v0

v1 whole, which is shorter than its diff:
```python
import functools
import math

import jax
import jax.numpy as jnp
from jax import lax
from jax.experimental import pallas as pl
from jax.experimental.pallas import tpu as pltpu
from jax.sharding import PartitionSpec as P

BF = jnp.bfloat16
F32 = jnp.float32
T = 128
NT = 8
ROWS = NT * T
VMEM_LIMIT = 40 * 1024 * 1024


def swap_in(block):
    count = lax.axis_size("wide")
    return lax.ppermute(
        block, "wide", [p for i in range(0, count - 1, 2) for p in ((i, i + 1), (i + 1, i))]
    )


def swap_out(block):
    count = lax.axis_size("wide")
    return lax.ppermute(
        block, "wide", [p for i in range(1, count - 1, 2) for p in ((i, i + 1), (i + 1, i))]
    )


def exchange_forward(pay_in, pay_out):
    got_in = swap_in(pay_in)
    got_out = swap_out(jnp.concatenate([pay_out, got_in[:1]], axis=0))
    return got_in, got_out, swap_in(got_out)


def exchange_back(pay_in, pay_out):
    got_in = swap_in(pay_in)
    got_out = swap_out(
        jnp.concatenate([pay_out[:1] + got_in[3:], pay_out[1:]], axis=0)
    )
    return got_in, got_out, swap_in(got_out)


def dot(a, b):
    return jnp.dot(a, b, preferred_element_type=F32)


def dot_nt(a, b):
    return lax.dot_general(a, b, (((1,), (1,)), ((), ())), preferred_element_type=F32)


def dot_tn(a, b):
    return lax.dot_general(a, b, (((0,), (0,)), ((), ())), preferred_element_type=F32)


def tile(ref, i):
    start = i * T if isinstance(i, int) else pl.multiple_of(i * T, T)
    return ref.at[pl.ds(start, T)]


class Place:
    def __init__(self, meta):
        self.idx = lambda r, s: meta[4 * r + s]
        core = meta[32]
        self.e_in = 7 - 7 * core
        self.n_in = 6 - 5 * core
        self.e_out = 7 * core
        self.n_out = 1 + 5 * core
        self.pos_in = 9 - 9 * core
        self.pos_out = 9 * core
        row_in = jnp.where(core == 0, meta[4 * 7 + 3], meta[3])
        row_out = jnp.where(core == 0, meta[3], meta[4 * 7 + 3])
        self.t_in = jnp.clip(row_in - 1, 0, NT - 1)
        self.t_out = jnp.clip(row_out - 1, 0, NT - 1)


def write_forward_payload(place, own, pay_in, pay_out, lanes):
    for j, i in enumerate((place.e_in, place.n_in, place.t_in)):
        pay_in[j, :, lanes] = tile(own, i)[...]
    for j, i in enumerate((place.e_out, place.n_out, place.t_out)):
        pay_out[j, :, lanes] = tile(own, i)[...]


def forward_row(place, vfg, src, r):
    low = tile(src, place.idx(0, 1))[...] if r == 0 else tile(src, r)[...]
    high = tile(src, place.idx(7, 2))[...] if r == 7 else tile(src, r + 2)[...]
    picked = jnp.concatenate(
        [low, tile(src, r + 1)[...], high, tile(src, place.idx(r, 3))[...]], axis=0
    )
    return dot(vfg[r], picked)


def lanes_of(vals):
    return jnp.concatenate([vals[k] for k in range(6)], axis=1)


def first_order(place, vfg, vin, vout, zext, d1, rin, rout, rfwd):
    tile(zext, place.pos_in)[...] = rin[0]
    tile(zext, place.pos_out)[...] = rout[0]
    for r in range(NT):
        tile(d1, r + 1)[...] = forward_row(place, vfg, zext, r).astype(BF)
    edge = tile(zext, place.e_in + 1)[...]
    picked = jnp.concatenate([rin[0], rin[1], edge, edge, rin[2], rfwd[0]], axis=0)
    tile(d1, place.pos_in)[...] = dot(lanes_of(vin), picked).astype(BF)
    edge = tile(zext, place.e_out + 1)[...]
    picked = jnp.concatenate([rout[0], rout[1], edge, edge, rout[2], rout[3]], axis=0)
    tile(d1, place.pos_out)[...] = dot(lanes_of(vout), picked).astype(BF)


def second_order(place, vfg, zext, d1, r):
    z = tile(zext, r + 1)[...].astype(F32)
    return (2.0 * forward_row(place, vfg, d1, r) - z).astype(BF)


def write_state_payload(place, st, x, pay_in, pay_out):
    for pay, tiles in (
        (pay_in, (place.e_in, place.n_in, place.t_in)),
        (pay_out, (place.e_out, place.n_out, place.t_out)),
    ):
        for j, i in enumerate(tiles):
            pay[j, :, :T] = tile(st, i)[...].astype(BF)
            pay[j, :, T:] = tile(x, i)[...]


def prepare_kernel(
    meta, counts, order, inputs, state, cot, vals,
    x0, x1, x2, c0, c1, c2, st, pay_in, pay_out, vfg, vbg, vbd, sb,
):
    place = Place(meta)
    rest = state[...]
    for k in range(3):
        part = rest.astype(BF)
        sb[k] = part
        rest = rest - part.astype(F32)
    lane = lax.broadcasted_iota(jnp.int32, (T, T), 1)
    for j in range(NT):
        wanted = jnp.broadcast_to(order[j : j + 1, :].astype(F32), (T, T)).T.astype(jnp.int32)
        pick = jnp.concatenate(
            [(wanted == lane + k * T).astype(F32).astype(BF) for k in range(NT)], axis=1
        )
        rows = slice(j * T, (j + 1) * T)
        for k, (x_out, c_out) in enumerate(((x0, c0), (x1, c1), (x2, c2))):
            x_out[rows] = dot(pick, inputs[k]).astype(BF)
            c_out[rows] = dot(pick, cot[k]).astype(BF)
        st[rows] = dot(pick, sb[0]) + dot(pick, sb[1]) + dot(pick, sb[2])
    write_state_payload(place, st, x0, pay_in, pay_out)
    for r in range(NT):
        live = (counts[r] > 3).astype(F32)
        last = (vals[r, 3].astype(F32) * live).astype(BF)
        vfg[r, :, 0:T] = vals[r, 1]
        vfg[r, :, T : 2 * T] = vals[r, 0]
        vfg[r, :, 2 * T : 3 * T] = vals[r, 2]
        vfg[r, :, 3 * T :] = last
        vbg[r, :, T : 2 * T] = vals[r, 0].T
        if r > 0:
            vbg[r - 1, :, 2 * T :] = vals[r, 1].T
        else:
            vbd[8] = vals[r, 1].T
        if r < NT - 1:
            vbg[r + 1, :, 0:T] = vals[r, 2].T
        else:
            vbd[9] = vals[r, 2].T
        vbd[r] = last.T
    vbg[0, :, 0:T] = jnp.zeros((T, T), BF)
    vbg[NT - 1, :, 2 * T :] = jnp.zeros((T, T), BF)


def transposed_kernel(vin, vout, vin_t, vout_t):
    for k in range(6):
        vin_t[k] = vin[k].T
        vout_t[k] = vout[k].T


def gate_kernel(
    meta, st, x, rin, rout, rfwd, vfg, vin, vout, gw, gb, cw, cb,
    feats, r_out, u_out, q_out, xc_out, pay_in, pay_out, zext, d1,
):
    place = Place(meta)
    zext[T : T + ROWS, :T] = st[...].astype(BF)
    zext[T : T + ROWS, T:] = x[...]
    first_order(place, vfg, vin, vout, zext, d1, rin, rout, rfwd)
    for r in range(NT):
        d2 = second_order(place, vfg, zext, d1, r)
        z = tile(zext, r + 1)[...]
        one = tile(d1, r + 1)[...]
        row = jnp.concatenate(
            [z[:, T:], one[:, T:], d2[:, T:], z[:, :T], one[:, :T], d2[:, :T]], axis=1
        )
        tile(feats, r)[...] = row
    for h in range(4):
        rows = slice(h * 256, (h + 1) * 256)
        f = feats[rows]
        pre = dot(f, gw[...]) + gb[...]
        xc_out[rows] = dot(f[:, : 3 * T], cw[: 3 * T]) + cb[...]
        reset = jax.nn.sigmoid(pre[:, :T])
        r_out[rows] = reset
        u_out[rows] = jax.nn.sigmoid(pre[:, T:])
        q_out[rows] = (reset * st[rows]).astype(BF)
    write_forward_payload(place, q_out, pay_in, pay_out, slice(0, T))


def cand_kernel(
    meta, q, rin, rout, rfwd, vfg, vin, vout, cw, xc, u, st, *rest, last
):
    if last:
        fq, c_out, zext, d1 = rest
    else:
        x_next, fq, c_out, st_out, pay_in, pay_out, zext, d1 = rest
    place = Place(meta)
    zext[T : T + ROWS] = q[...]
    first_order(place, vfg, vin, vout, zext, d1, rin, rout, rfwd)
    for r in range(NT):
        d2 = second_order(place, vfg, zext, d1, r)
        tile(fq, r)[...] = jnp.concatenate(
            [tile(zext, r + 1)[...], tile(d1, r + 1)[...], d2], axis=1
        )
    for h in range(4):
        rows = slice(h * 256, (h + 1) * 256)
        cand = jnp.tanh(dot(fq[rows], cw[3 * T :]) + xc[rows])
        c_out[rows] = cand
        if not last:
            st_out[rows] = u[rows] * st[rows] + (1.0 - u[rows]) * cand
    if not last:
        write_state_payload(place, st_out, x_next, pay_in, pay_out)


def add_received(place, acc, rin, rout, rfwd):
    for i, block in (
        (place.e_in, rin[0]),
        (place.n_in, rin[1]),
        (place.t_in, rin[2]),
        (place.e_out, rout[0]),
        (place.n_out, rout[1]),
        (place.t_out, rout[2]),
        (place.e_in, rfwd[3]),
    ):
        tile(acc, i)[...] += block.astype(F32)


def back_rows(place, vbg, vbd, y, acc, base):
    zero = jnp.zeros((T, acc.shape[1]), F32)
    tile(acc, 0)[...] = zero
    tile(acc, 9)[...] = zero
    for r in range(NT):
        lo, hi = max(r - 1, 0), min(r + 2, NT)
        lhs = vbg[r, :, (lo - r + 1) * T : (hi - r + 1) * T]
        tile(acc, r + 1)[...] = base(r, dot(lhs, y[lo * T : hi * T]))
    parts = [(place.idx(0, 1), 8, 0), (place.idx(7, 2), 9, 7)]
    parts += [(place.idx(r, 3), r, r) for r in range(NT)]
    for i, k, r in parts:
        tile(acc, i)[...] += dot(vbd[k], y[r * T : (r + 1) * T])


def diffuse_back(place, vbg, vbd, vin_t, vout_t, a, wide, y, w, acc, pay_in, pay_out):
    for r in range(NT):
        rows = slice(r * T, (r + 1) * T)
        y[rows] = a(2, rows).astype(BF)
    back_rows(
        place, vbg, vbd, y, acc, lambda r, v: a(1, slice(r * T, (r + 1) * T)) * 0.5 + v
    )
    for e in range(NT + 2):
        tile(w, e)[...] = (2.0 * tile(acc, e)[...]).astype(BF)
    own = w.at[pl.ds(T, ROWS)]

    def second(r, v):
        rows = slice(r * T, (r + 1) * T)
        return a(0, rows) - a(2, rows) + v

    back_rows(place, vbg, vbd, own, acc, second)
    for pos, edge, vals, pay in (
        (place.pos_in, place.e_in, vin_t, pay_in),
        (place.pos_out, place.e_out, vout_t, pay_out),
    ):
        got = dot(vals[...].reshape(6 * T, T), tile(w, pos)[...])
        part = [got[k * T : (k + 1) * T] for k in range(6)]
        tile(acc, edge + 1)[...] += part[2] + part[3]
        pay[0] = (tile(acc, pos)[...] + part[0]).astype(BF)
        pay[1] = part[1].astype(BF)
        pay[2] = part[4].astype(BF)
        pay[3] = part[5].astype(BF)


def cand_back_kernel(*refs, first):
    refs = list(refs)
    take = lambda n: [refs.pop(0) for _ in range(n)]
    meta, cot, u, c, st, feats, fq, cw, vbg, vbd, vin_t, vout_t = take(12)
    if not first:
        gs_part, gx_part, rin, rout, rfwd, wc_in = take(6)
    gp_out, ec_out, eu_out, gq_out, wc_out, pay_in, pay_out = take(7)
    if not first:
        (gx_out,) = take(1)
    gs, g, y, w, acc = take(5)
    place = Place(meta)
    if not first:
        gs[:, :T] = gs_part[...]
        gs[:, T:] = gx_part[...]
        add_received(place, gs, rin, rout, rfwd)
        gx_out[...] = gs[:, T:].astype(BF)
    sum_c = jnp.zeros((1, T), F32)
    sum_u = jnp.zeros((1, T), F32)
    for h in range(NT):
        rows = slice(h * T, (h + 1) * T)
        grad = cot[rows].astype(F32)
        if not first:
            grad = grad + gs[rows, :T]
        upd, cand = u[rows], c[rows]
        pre = grad * (1.0 - upd) * (1.0 - cand * cand)
        gate = grad * (st[rows] - cand) * upd * (1.0 - upd)
        gp_out[rows] = grad * upd
        ec_out[rows] = pre.astype(BF)
        eu_out[rows] = gate.astype(BF)
        sum_c = sum_c + jnp.sum(pre, axis=0, keepdims=True)
        sum_u = sum_u + jnp.sum(gate, axis=0, keepdims=True)
    ec = ec_out[...]
    g[...] = dot_nt(ec, cw[3 * T :])
    diffuse_back(
        place, vbg, vbd, vin_t, vout_t,
        lambda k, rows: g[rows, k * T : (k + 1) * T],
        T, y, w, acc, pay_in, pay_out,
    )
    gq_out[...] = acc[T : T + ROWS]
    low = dot_tn(ec, feats[:, : 3 * T])
    high = dot_tn(ec, fq[...])
    sums = jnp.concatenate([sum_c, sum_u, jnp.zeros((1, 4 * T), F32)], axis=1)
    sums = jnp.concatenate([sums, jnp.zeros((7, 6 * T), F32)], axis=0)
    if not first:
        low = low + wc_in[:T, : 3 * T]
        high = high + wc_in[:T, 3 * T :]
        sums = sums + wc_in[T:]
    wc_out[:T, : 3 * T] = low
    wc_out[:T, 3 * T :] = high
    wc_out[T:] = sums


def gate_back_kernel(*refs, first):
    refs = list(refs)
    take = lambda n: [refs.pop(0) for _ in range(n)]
    meta, gq_part, rin, rout, rfwd, gp, r_ref, st, ec, eu, feats, gw, cw = take(13)
    vbg, vbd, vin_t, vout_t = take(4)
    if not first:
        (wg_in,) = take(1)
    gs_out, gx_out, wg_out, pay_in, pay_out = take(5)
    gq, eg, gps, g, y, w, acc = take(7)
    place = Place(meta)
    gq[...] = gq_part[...]
    add_received(place, gq, rin, rout, rfwd)
    sum_r = jnp.zeros((1, T), F32)
    for h in range(NT):
        rows = slice(h * T, (h + 1) * T)
        grad, reset = gq[rows], r_ref[rows]
        gps[rows] = gp[rows] + grad * reset
        pre = grad * st[rows] * reset * (1.0 - reset)
        eg[rows, :T] = pre.astype(BF)
        eg[rows, T:] = eu[rows]
        sum_r = sum_r + jnp.sum(pre, axis=0, keepdims=True)
    e = eg[...]
    for k in range(3):
        cols = slice(2 * k * T, (2 * k + 1) * T)
        g[:, cols] = dot_nt(e, gw[(3 + k) * T : (4 + k) * T])
        cols = slice((2 * k + 1) * T, (2 * k + 2) * T)
        g[:, cols] = dot_nt(e, gw[k * T : (k + 1) * T]) + dot_nt(
            ec[...], cw[k * T : (k + 1) * T]
        )
    diffuse_back(
        place, vbg, vbd, vin_t, vout_t,
        lambda k, rows: g[rows, 2 * k * T : 2 * (k + 1) * T],
        2 * T, y, w, acc, pay_in, pay_out,
    )
    gs_out[...] = acc[T : T + ROWS, :T] + gps[...]
    gx_out[...] = acc[T : T + ROWS, T:]
    total = dot_tn(e, feats[...])
    sums = jnp.concatenate([sum_r, jnp.zeros((1, 5 * T), F32)], axis=1)
    sums = jnp.concatenate([sums, jnp.zeros((7, 6 * T), F32)], axis=0)
    if not first:
        total = total + wg_in[: 2 * T]
        sums = sums + wg_in[2 * T :]
    wg_out[: 2 * T] = total
    wg_out[2 * T :] = sums


def finish_kernel(
    meta, order, gs_part, gx_part, rin, rout, rfwd, gx1, gx2, gi_out, gs_out, gs, parts
):
    place = Place(meta)
    gs[:, :T] = gs_part[...]
    gs[:, T:] = gx_part[...]
    add_received(place, gs, rin, rout, rfwd)
    rest = gs[:, :T]
    for k in range(3):
        part = rest.astype(BF)
        parts[:, k * T : (k + 1) * T] = part
        rest = rest - part.astype(F32)
    parts[:, 3 * T : 4 * T] = gs[:, T:].astype(BF)
    parts[:, 4 * T : 5 * T] = gx1[...]
    parts[:, 5 * T :] = gx2[...]
    row = lax.broadcasted_iota(jnp.int32, (T, T), 0)
    for k in range(NT):
        put = jnp.concatenate(
            [
                (jnp.broadcast_to(order[j : j + 1, :], (T, T)) == row + k * T)
                .astype(F32)
                .astype(BF)
                for j in range(NT)
            ],
            axis=1,
        )
        rows = slice(k * T, (k + 1) * T)
        got = dot(put, parts[...])
        gs_out[rows] = got[:, :T] + got[:, T : 2 * T] + got[:, 2 * T : 3 * T]
        for t in range(3):
            gi_out[t, rows] = got[:, (3 + t) * T : (4 + t) * T].astype(BF)


SMEM = pl.BlockSpec(memory_space=pltpu.SMEM)
VMEM = pl.BlockSpec(memory_space=pltpu.VMEM)


def run(kernel, name, smem, args, outs, scratch=()):
    specs = [SMEM if i in smem else VMEM for i in range(len(args))]
    out_shape = [jax.ShapeDtypeStruct(s, d) for s, d in outs]
    return pl.pallas_call(
        kernel,
        name=name,
        in_specs=specs,
        out_specs=[VMEM] * len(outs),
        out_shape=out_shape,
        scratch_shapes=[pltpu.VMEM(s, d) for s, d in scratch],
        compiler_params=pltpu.CompilerParams(vmem_limit_bytes=VMEM_LIMIT),
    )(*args)


def edge_values(tile_vals, local_cols, tile_counts, row, low_side, pos_them, pos_far):
    vals = lax.dynamic_index_in_dim(tile_vals, row, 0, keepdims=False)
    col = lax.dynamic_index_in_dim(local_cols, row, 0, keepdims=False)[3]
    live = lax.dynamic_index_in_dim(tile_counts, row, 0, keepdims=False) > 3
    ahead = jnp.where(low_side, vals[1], vals[2])
    inside = jnp.where(low_side, vals[2], vals[1])
    them, far = col == pos_them, col == pos_far
    zero = jnp.zeros_like(vals[3])
    return jnp.stack(
        [
            vals[0],
            inside,
            ahead,
            jnp.where(live & them, vals[3], zero),
            jnp.where(live & ~them & ~far, vals[3], zero),
            jnp.where(live & far, vals[3], zero),
        ]
    )


def per_device(
    inputs, state_init, cotangent, gate_w, gate_b, cand_w, cand_b,
    tile_vals, tile_cols, tile_counts, sector_order,
):
    device = lax.axis_index("wide")
    core = device % 2
    local_cols = tile_cols - (device * NT - 1)
    meta = jnp.concatenate([local_cols.reshape(-1), core[None]]).astype(jnp.int32)
    order = sector_order.reshape(NT, T)
    gb = gate_b.reshape(1, -1)
    cb = cand_b.reshape(1, -1)
    e_in, e_out = 7 - 7 * core, 7 * core
    p_in, p_out = 9 - 9 * core, 9 * core
    vin = swap_in(
        edge_values(tile_vals, local_cols, tile_counts, e_in, core == 1, p_in, p_out)
    )
    vout = swap_out(
        edge_values(tile_vals, local_cols, tile_counts, e_out, core == 0, p_out, p_in)
    )
    big = (ROWS, T)
    x0, x1, x2, c0, c1, c2, st, pay_in, pay_out, vfg, vbg, vbd = run(
        prepare_kernel,
        "prepare",
        (0, 1),
        (meta, tile_counts, order, inputs, state_init, cotangent, tile_vals),
        [(big, BF)] * 6
        + [(big, F32), ((3, T, 2 * T), BF), ((3, T, 2 * T), BF)]
        + [((NT, T, 4 * T), BF), ((NT, T, 3 * T), BF), ((NT + 2, T, T), BF)],
        [((3,) + big, BF)],
    )
    pay = (pay_in, pay_out)
    vin_t, vout_t = run(
        transposed_kernel, "turn", (), (vin, vout), [((6, T, T), BF)] * 2
    )
    xs, cots = (x0, x1, x2), (c0, c1, c2)
    saved = []
    steps = inputs.shape[0]
    wide = ((NT + 2) * T, 2 * T)
    slim = ((NT + 2) * T, T)
    for t in range(steps):
        rin, rout, rfwd = exchange_forward(*pay)
        feats, r, u, q, xc, *pay = run(
            gate_kernel,
            "gate",
            (0,),
            (meta, st, xs[t], rin, rout, rfwd, vfg, vin, vout, gate_w, gb, cand_w, cb),
            [((ROWS, 6 * T), BF), (big, F32), (big, F32), (big, BF), (big, F32)]
            + [((3, T, T), BF)] * 2,
            [(wide, BF)] * 2,
        )
        rin, rout, rfwd = exchange_forward(*pay)
        last = t == steps - 1
        got = run(
            functools.partial(cand_kernel, last=last),
            "cand",
            (0,),
            (meta, q, rin, rout, rfwd, vfg, vin, vout, cand_w, xc, u, st)
            + (() if last else (xs[t + 1],)),
            [((ROWS, 3 * T), BF), (big, F32)]
            + ([] if last else [(big, F32)] + [((3, T, 2 * T), BF)] * 2),
            [(slim, BF)] * 2,
        )
        saved.append((st, feats, r, u, got[0], got[1]))
        if not last:
            st, pay = got[2], got[3:]
    ops = (vbg, vbd, vin_t, vout_t)
    gxs = [None] * steps
    carry = ()
    wg = ()
    for t in reversed(range(steps)):
        st, feats, r, u, fq, c = saved[t]
        first = t == steps - 1
        got = run(
            functools.partial(cand_back_kernel, first=first),
            "cand_back",
            (0,),
            (meta, cots[t], u, c, st, feats, fq, cand_w) + ops + carry,
            [(big, F32), (big, BF), (big, BF), (big, F32), ((T + 8, 6 * T), F32)]
            + [((4, T, T), BF)] * 2
            + ([] if first else [(big, BF)]),
            [((ROWS, 2 * T), F32), ((ROWS, 3 * T), F32), (big, BF), (slim, BF), (slim, F32)],
        )
        gp, ec, eu, gq, wc, *pay = got[:7]
        if not first:
            gxs[t + 1] = got[7]
        rin, rout, rfwd = exchange_back(*pay)
        gs_part, gx_part, wg_new, *pay = run(
            functools.partial(gate_back_kernel, first=first),
            "gate_back",
            (0,),
            (meta, gq, rin, rout, rfwd, gp, r, st, ec, eu, feats, gate_w, cand_w) + ops + wg,
            [(big, F32), (big, F32), ((2 * T + 8, 6 * T), F32)] + [((4, T, 2 * T), BF)] * 2,
            [
                (big, F32), ((ROWS, 2 * T), BF), (big, F32), ((ROWS, 6 * T), F32),
                ((ROWS, 2 * T), BF), (wide, BF), (wide, F32),
            ],
        )
        wg = (wg_new,)
        rin, rout, rfwd = exchange_back(*pay)
        carry = (gs_part, gx_part, rin, rout, rfwd, wc)
    grads = lax.psum(jnp.concatenate([wg[0], wc], axis=0), "wide")
    gi, gs = run(
        finish_kernel,
        "finish",
        (0,),
        (meta, order, gs_part, gx_part, rin, rout, rfwd, gxs[1], gxs[2]),
        [((steps,) + big, BF), (big, F32)],
        [((ROWS, 2 * T), F32), ((ROWS, 6 * T), BF)],
    )
    scale = 1.0 / math.sqrt(ROWS * lax.axis_size("wide") * steps)
    grads = grads * scale
    wgt, bg, wct, bc = grads[: 2 * T], grads[2 * T], grads[2 * T + 8 : 3 * T + 8], grads[3 * T + 8]
    return (
        gi,
        gs,
        wgt.T,
        jnp.concatenate([bg[:T], bc[T : 2 * T]]),
        wct.T,
        bc[:T],
    )


def solution(mesh):
    return jax.shard_map(
        per_device,
        mesh=mesh,
        in_specs=(
            P(None, ("parts", "wide"), None),
            P(("parts", "wide"), None),
            P(None, ("parts", "wide"), None),
            P(),
            P(),
            P(),
            P(),
            P(("parts", "wide"), None, None, None),
            P(("parts", "wide"), None),
            P(("parts", "wide")),
            P(("parts", "wide")),
        ),
        out_specs=(
            P(None, ("parts", "wide"), None),
            P(("parts", "wide"), None),
            P("parts", None),
            P("parts"),
            P("parts", None),
            P("parts"),
        ),
        check_vma=False,
    )
```

time: 709 us -> 333 us (0.47); the launches traced: 695 us -> 332 us
  other arithmetic: 151 us -> 18 us
  starting transfers between devices: 233 us -> 123 us
  matrix products: 103 us -> 0 us
  local copies, waits for them, and re-layouts: 125 us -> 24.7 us
  waiting for transfers between devices: 29.1 us -> 105 us
  Pallas kernels: 0 us -> 42.8 us
  blocking collectives: 36.1 us -> 0 us
    ppermute x72 -> x38, starting transfers between devices: 233 us -> 123 us  [the longest x25 113 us: swap_in(): lax.ppermute(block, 'wide', [p for i in range(0, count - 1, 2) for p in (...]
    dot_general x54 -> x0, matrix products: 103 us -> none  [the longest x18 34.9 us: backward(): jnp.einsum('rsab,raf->rsbf', masked, grads.reshape(tiles_here, tile_width...]
    scatter-add x54 -> x0, other arithmetic: 96.6 us -> none  [the longest x18 83.9 us: backward(): extended = jnp.zeros((tiles_here + 2, tile_width, feat_count), jnp.float3...]
    psum x1, waiting for transfers between devices: 22.1 us -> 83.1 us  [per_device(): grads = lax.psum(jnp.concatenate([wg[0], wc], axis=0), 'wide')]
    gather x21 -> x0, local copies, waits for them, and re-layouts: 47.8 us -> none  [the longest x18 30.8 us: forward(): picked = extended[local_cols]]
    pallas_call x0 -> x15, Pallas kernels: none -> 42.8 us  [run(): pl.pallas_call(kernel, name=name, in_specs=specs, out_specs=[VMEM] * len(...]
    psum x1 -> x0, blocking collectives: 36.1 us -> none  [per_device(): lax.psum((total_gw, total_gb, total_cw, total_cb), 'wide')]
    scatter x1 -> x0, local copies, waits for them, and re-layouts: 26.6 us -> none  [per_device(): grad_inputs = jnp.zeros((steps_count, row_count, hidden), jnp.bfloat16).a...]
  transfers between devices with their start and end apart: 73 -> 39, of which waited for: 15 -> 23; matrix products, arithmetic and copies ran while one was open for 27% -> 8% of each run, Pallas kernels for 0% -> 0%
where the time goes in v1:
time: 333 us; the launch traced here: 332 us
  starting transfers between devices  123 us (37%)
  waiting for transfers between devices  105 us (32%)
  Pallas kernels  42.8 us (13%)
  local copies, waits for them, and re-layouts  24.7 us (7%)
  between operations  18.5 us (6%)
  other arithmetic  18 us (5%)
    ppermute x25, starting transfers between devices, swap_in(): lax.ppermute(block, 'wide', [p for i in range(0, count - 1, 2) for p in (...  113 us
    psum x1, waiting for transfers between devices, per_device(): grads = lax.psum(jnp.concatenate([wg[0], wc], axis=0), 'wide')  83.1 us
    pallas_call x15, Pallas kernels, run(): pl.pallas_call(kernel, name=name, in_specs=specs, out_specs=[VMEM] * len(...  42.8 us
    ppermute x25, waiting for transfers between devices, swap_in(): lax.ppermute(block, 'wide', [p for i in range(0, count - 1, 2) for p in (...  21.8 us
    unnamed x59, local copies, waits for them, and re-layouts  15.8 us
    ppermute x13, starting transfers between devices, swap_out(): lax.ppermute(block, 'wide', [p for i in range(1, count - 1, 2) for p in (...  9.82 us
    unnamed x6, other arithmetic  8.37 us
  transfers between devices with their start and end apart: 39, of which 23 were waited for; matrix products, arithmetic and copies ran while one was open for 8% of the time, Pallas kernels for 0%

profile of v1, /device:TPU:0, one launch (start us, length us, event | category | flops | bytes accessed | tf_op | source)
XLA Modules:
  0.0 331.7 jit_solution(5945761605352874216)
XLA Ops:
  8.5 1.2 copy-done.2
  14.4 6.6 %prepare.1 = (bf16[1024,128]{1,0:T(8,128)(2,1)S(1)}, bf16[1024,128]{1,0:T(8,128)(2,1)S(1)}, bf16[1024,128]{1,0:T(8,128)(2,1)S(1)}, bf16[1024,128]{1,0:T(8,128)(2...) custom-call(s32[33]{0:T(128)S(1)} %pad_add_fusion.meta.refs_0_, ...), custom_call_target="tpu_custom_call" | custom-call | tf_op jit(solution)/shard_map/prepare/pallas_call | solution.py:424
  26.3 1.4 constant_dynamic-slice_fusion
  27.7 1.4 fusion
  29.1 1.2 slice.164
  32.2 1.4 bitcast_dynamic-update-slice_fusion.4
  33.6 1.4 bitcast_dynamic-update-slice_fusion.3
  35.0 1.4 bitcast_dynamic-update-slice_fusion.2
  36.4 1.4 bitcast_dynamic-update-slice_fusion.1
  38.6 1.7 pad_maximum_fusion.1
  40.3 1.4 collective-permute-start.1
  41.6 1.4 bitcast_dynamic-update-slice_fusion.8
  45.5 1.4 bitcast_dynamic-update-slice_fusion.7
  46.9 1.4 bitcast_dynamic-update-slice_fusion
  48.3 3.2 collective-permute-start.2
  51.5 1.4 bitcast_dynamic-update-slice_fusion.5
  55.5 2.8 gate.3
  58.4 8.1 %collective-permute-start.5 = (bf16[3,128,128]{2,1,0:T(8,128)(2,1)S(1)}, bf16[3,128,128]{2,1,0:T(8,128)(2,1)S(1)}, u32[]{:S(2)}, u32[]{:S(2)}) collective-permute-start(bf16[3,128,128]{2,1,0:T(8,128)(2,1)S(1)} %get-tuple-element.101), channel_id=1, source_target_pairs={{0,1},{1,0},{2,3},{3,2},{4,5},{5,4},{6,7},{7,6},{8,9},{9,8},{10,11... | collective-permute-start | bytes 294920 | tf_op jit(solution)/shard_map/ppermute | solution.py:21
  68.1 6.6 %collective-permute-start.7 = (bf16[4,128,128]{2,1,0:T(8,128)(2,1)S(1)}, bf16[4,128,128]{2,1,0:T(8,128)(2,1)S(1)}, u32[]{:S(2)}, u32[]{:S(2)}) collective-permute-start(bf16[4,128,128]{2,1,0:T(8,128)(2,1)S(1)} %collective-permute-done.6.rout), channel_id=1, source_target_pairs={{0,1},{1,0},{2,3},{3,2},{4,5},{5,4},{6,7},{7,6},{8,9},{9,8},{10,11... | collective-permute-start | bytes 393224 | tf_op jit(solution)/shard_map/ppermute | solution.py:21
  75.7 1.8 cand.3
  79.8 10.8 %collective-permute-start.10 = (bf16[4,128,256]{2,1,0:T(8,128)(2,1)S(1)}, bf16[4,128,256]{2,1,0:T(8,128)(2,1)S(1)}, u32[]{:S(2)}, u32[]{:S(2)}) collective-permute-start(bf16[4,128,256]{2,1,0:T(8,128)(2,1)S(1)} %collective-permute-done.9.rout), channel_id=1, source_target_pairs={{0,1},{1,0},{2,3},{3,2},{4,5},{5,4},{6,7},{7,6},{8,9},{9,8},{10,11... | collective-permute-start | bytes 786440 | tf_op jit(solution)/shard_map/ppermute | solution.py:21
  90.6 1.2 collective-permute-done.10.rfwd
  91.8 2.3 gate.4
  96.3 6.7 %collective-permute-start.13 = (bf16[4,128,128]{2,1,0:T(8,128)(2,1)S(1)}, bf16[4,128,128]{2,1,0:T(8,128)(2,1)S(1)}, u32[]{:S(2)}, u32[]{:S(2)}) collective-permute-start(bf16[4,128,128]{2,1,0:T(8,128)(2,1)S(1)} %collective-permute-done.12.rout), channel_id=1, source_target_pairs={{0,1},{1,0},{2,3},{3,2},{4,5},{5,4},{6,7},{7,6},{8,9},{9,8},{10,11... | collective-permute-start | bytes 393224 | tf_op jit(solution)/shard_map/ppermute | solution.py:21
  104.0 1.8 cand.4
  108.1 10.6 %collective-permute-start.16 = (bf16[4,128,256]{2,1,0:T(8,128)(2,1)S(1)}, bf16[4,128,256]{2,1,0:T(8,128)(2,1)S(1)}, u32[]{:S(2)}, u32[]{:S(2)}) collective-permute-start(bf16[4,128,256]{2,1,0:T(8,128)(2,1)S(1)} %collective-permute-done.15.rout), channel_id=1, source_target_pairs={{0,1},{1,0},{2,3},{3,2},{4,5},{5,4},{6,7},{7,6},{8,9},{9,8},{10,11... | collective-permute-start | bytes 786440 | tf_op jit(solution)/shard_map/ppermute | solution.py:21
  119.9 2.3 gate.5
  124.3 6.7 %collective-permute-start.19 = (bf16[4,128,128]{2,1,0:T(8,128)(2,1)S(1)}, bf16[4,128,128]{2,1,0:T(8,128)(2,1)S(1)}, u32[]{:S(2)}, u32[]{:S(2)}) collective-permute-start(bf16[4,128,128]{2,1,0:T(8,128)(2,1)S(1)} %collective-permute-done.18.rout), channel_id=1, source_target_pairs={{0,1},{1,0},{2,3},{3,2},{4,5},{5,4},{6,7},{7,6},{8,9},{9,8},{10,11... | collective-permute-start | bytes 393224 | tf_op jit(solution)/shard_map/ppermute | solution.py:21
  132.0 1.7 cand.5
  133.8 2.3 cand_back.3
  138.2 7.4 %collective-permute-start.22 = (bf16[4,128,128]{2,1,0:T(8,128)(2,1)S(1)}, bf16[4,128,128]{2,1,0:T(8,128)(2,1)S(1)}, u32[]{:S(2)}, u32[]{:S(2)}) collective-permute-start(bf16[4,128,128]{2,1,0:T(8,128)(2,1)S(1)} %collective-permute-done.21.refs_3_), channel_id=1, source_target_pairs={{0,1},{1,0},{2,3},{3,2},{4,5},{5,4},{6,7},{7,6},{8,9},{9,8},{10,11... | collective-permute-start | bytes 393224 | tf_op jit(solution)/shard_map/ppermute | solution.py:21
  146.5 4.0 %gate_back.3 = (f32[1024,128]{1,0:T(8,128)S(1)}, f32[1024,128]{1,0:T(8,128)S(1)}, f32[264,768]{1,0:T(8,128)S(1)}, bf16[4,128,256]{2,1,0:T(8,128)(2,1)S(1)}, bf16[4,128,256]{2,1,0:T(8,128)(2,1)S(1)}) custom-call(s32[33]{0:T(128)S(1)} %pad_add_fusion.meta.refs_0_, f32[1024,128]{1,0:T(8,128)S(1)} %get-tuple-element.137.refs_1_, ...), custom_call_target="tpu_custom_call" | custom-call | tf_op jit(solution)/shard_map/gate_back/pallas_call | solution.py:424
  152.9 10.8 %collective-permute-start.25 = (bf16[4,128,256]{2,1,0:T(8,128)(2,1)S(1)}, bf16[4,128,256]{2,1,0:T(8,128)(2,1)S(1)}, u32[]{:S(2)}, u32[]{:S(2)}) collective-permute-start(bf16[4,128,256]{2,1,0:T(8,128)(2,1)S(1)} %collective-permute-done.24.refs_15_), channel_id=1, source_target_pairs={{0,1},{1,0},{2,3},{3,2},{4,5},{5,4},{6,7},{7,6},{8,9},{9,8},{10,11... | collective-permute-start | bytes 786440 | tf_op jit(solution)/shard_map/ppermute | solution.py:21
  164.9 2.5 cand_back.4
  169.8 6.5 %collective-permute-start.28 = (bf16[4,128,128]{2,1,0:T(8,128)(2,1)S(1)}, bf16[4,128,128]{2,1,0:T(8,128)(2,1)S(1)}, u32[]{:S(2)}, u32[]{:S(2)}) collective-permute-start(bf16[4,128,128]{2,1,0:T(8,128)(2,1)S(1)} %collective-permute-done.27.refs_3_), channel_id=1, source_target_pairs={{0,1},{1,0},{2,3},{3,2},{4,5},{5,4},{6,7},{7,6},{8,9},{9,8},{10,11... | collective-permute-start | bytes 393224 | tf_op jit(solution)/shard_map/ppermute | solution.py:21
  177.2 4.0 %gate_back.4 = (f32[1024,128]{1,0:T(8,128)S(1)}, f32[1024,128]{1,0:T(8,128)S(1)}, f32[264,768]{1,0:T(8,128)S(1)}, bf16[4,128,256]{2,1,0:T(8,128)(2,1)S(1)}, bf16[4,128,256]{2,1,0:T(8,128)(2,1)S(1)}) custom-call(s32[33]{0:T(128)S(1)} %pad_add_fusion.meta.refs_0_, f32[1024,128]{1,0:T(8,128)S(1)} %get-tuple-element.149.refs_1_, ...), custom_call_target="tpu_custom_call" | custom-call | tf_op jit(solution)/shard_map/gate_back/pallas_call | solution.py:424
  183.6 10.8 %collective-permute-start.31 = (bf16[4,128,256]{2,1,0:T(8,128)(2,1)S(1)}, bf16[4,128,256]{2,1,0:T(8,128)(2,1)S(1)}, u32[]{:S(2)}, u32[]{:S(2)}) collective-permute-start(bf16[4,128,256]{2,1,0:T(8,128)(2,1)S(1)} %collective-permute-done.30.refs_15_), channel_id=1, source_target_pairs={{0,1},{1,0},{2,3},{3,2},{4,5},{5,4},{6,7},{7,6},{8,9},{9,8},{10,11... | collective-permute-start | bytes 786440 | tf_op jit(solution)/shard_map/ppermute | solution.py:21
  195.6 2.5 cand_back.5
  200.3 6.7 %collective-permute-start.34 = (bf16[4,128,128]{2,1,0:T(8,128)(2,1)S(1)}, bf16[4,128,128]{2,1,0:T(8,128)(2,1)S(1)}, u32[]{:S(2)}, u32[]{:S(2)}) collective-permute-start(bf16[4,128,128]{2,1,0:T(8,128)(2,1)S(1)} %collective-permute-done.33.refs_3_), channel_id=1, source_target_pairs={{0,1},{1,0},{2,3},{3,2},{4,5},{5,4},{6,7},{7,6},{8,9},{9,8},{10,11... | collective-permute-start | bytes 393224 | tf_op jit(solution)/shard_map/ppermute | solution.py:21
  208.0 4.2 %gate_back.5 = (f32[1024,128]{1,0:T(8,128)S(1)}, f32[1024,128]{1,0:T(8,128)S(1)}, f32[264,768]{1,0:T(8,128)S(1)}, bf16[4,128,256]{2,1,0:T(8,128)(2,1)}, bf16[4,128,256]{2,1,0:T(8,128)(2,1)S(1)}) custom-call(s32[33]{0:T(128)S(1)} %pad_add_fusion.meta.refs_0_, f32[1024,128]{1,0:T(8,128)S(1)} %get-tuple-element.162.refs_1_, ...), custom_call_target="tpu_custom_call" | custom-call | tf_op jit(solution)/shard_map/gate_back/pallas_call | solution.py:424
  214.6 13.0 %collective-permute-start.37 = (bf16[4,128,256]{2,1,0:T(8,128)(2,1)S(1)}, bf16[4,128,256]{2,1,0:T(8,128)(2,1)S(1)}, u32[]{:S(2)}, u32[]{:S(2)}) collective-permute-start(bf16[4,128,256]{2,1,0:T(8,128)(2,1)S(1)} %collective-permute-done.36.rout), channel_id=1, source_target_pairs={{0,1},{1,0},{2,3},{3,2},{4,5},{5,4},{6,7},{7,6},{8,9},{9,8},{10,11... | collective-permute-start | bytes 786440 | tf_op jit(solution)/shard_map/ppermute | solution.py:21
  227.7 83.1 %all-reduce.2.cloned.1.call-done = f32[400,768]{1,0:T(8,128)} async-done(((f32[400,768]{1,0:T(8,128)}), f32[400,768]{1,0:T(8,128)}) %all-reduce.2.cloned.1.call-update) | async-done | bytes 1228816 | tf_op jit(solution)/shard_map/psum | solution.py:555
  310.8 2.5 broadcast_multiply_fusion
  313.2 1.8 slice_bitcast_fusion.1
  315.0 1.2 slice_bitcast_fusion
  317.4 1.9 copy.22
  319.3 1.2 slice_bitcast_fusion.2
  321.1 3.7 %finish.1 = (bf16[3,1024,128]{2,1,0:T(8,128)(2,1)}, f32[1024,128]{1,0:T(8,128)}) custom-call(s32[33]{0:T(128)S(1)} %pad_add_fusion.meta.refs_0_, s32[8,128]{1,0:T(8,128)S(1)} %bitcast.47, f32[1024,128]{1,0:T(8,128)S(1)} %get-tuple-element.170.gs_part, f32[1024,128]{1,0:T(8,128)S(1)} %get-tuple-element.171.gx_part, ...), custom_call_target="tpu_custom_call" | custom-call | tf_op jit(solution)/shard_map/finish/pallas_call | solution.py:424
  (157 shorter events, 50.4 us)
Async XLA Ops:
  7.2 303.6 %all-reduce.2.cloned.1.call-start = ((), (), s32[]{:S(2)}) async-start(), calls=%async_computation | async-start | bytes 2457600 | tf_op jit(solution)/shard_map/psum | solution.py:555
  25.2 29.4 %copy-start = (bf16[768,128]{1,0:T(8,128)(2,1)S(1)}, bf16[768,128]{1,0:T(8,128)(2,1)}, u32[]{:S(2)}) copy-start(bf16[768,128]{1,0:T(8,128)(2,1)} %refs_12_.5) | copy-start | bytes 589828
  25.2 29.4 %copy-start.1 = (bf16[768,256]{1,0:T(8,128)(2,1)S(1)}, bf16[768,256]{1,0:T(8,128)(2,1)}, u32[]{:S(2)}) copy-start(bf16[768,256]{1,0:T(8,128)(2,1)} %refs_11_.5) | copy-start | bytes 1179652
  25.2 29.4 %copy-start.23 = (f32[256]{0:T(256)S(1)}, f32[256]{0:T(256)}, u32[]{:S(2)}) copy-start(f32[256]{0:T(256)} %param.15) | copy-start | bytes 3076
  25.2 29.4 %copy-start.24 = (f32[128]{0:T(128)S(1)}, f32[128]{0:T(128)}, u32[]{:S(2)}) copy-start(f32[128]{0:T(128)} %param.17) | copy-start | bytes 1540
  25.2 12.6 %collective-permute-start = (bf16[3,128,256]{2,1,0:T(8,128)(2,1)}, bf16[3,128,256]{2,1,0:T(8,128)(2,1)}, u32[]{:S(2)}, u32[]{:S(2)}) collective-permute-start(bf16[3,128,256]{2,1,0:T(8,128)(2,1)} %get-tuple-element.96), channel_id=1, source_target_pairs={{0,1},{1,0},{2,3},{3,2},{4,5},{5,4},{6,7},{7,6},{8,9},{9,8},{10,11... | collective-permute-start | bytes 589832 | tf_op jit(solution)/shard_map/ppermute | solution.py:21
  40.3 8.0 %collective-permute-start.1 = (bf16[4,128,256]{2,1,0:T(8,128)(2,1)}, bf16[4,128,256]{2,1,0:T(8,128)(2,1)}, u32[]{:S(2)}, u32[]{:S(2)}) collective-permute-start(bf16[4,128,256]{2,1,0:T(8,128)(2,1)} %pad_maximum_fusion.1), channel_id=1, source_target_pairs={{1,2},{2,1},{3,4},{4,3},{5,6},{6,5},{7,8},{8,7},{9,10},{10,9},{11,... | collective-permute-start | bytes 786440 | tf_op jit(solution)/shard_map/ppermute | solution.py:28
  48.3 6.3 %collective-permute-start.2 = (bf16[4,128,256]{2,1,0:T(8,128)(2,1)}, bf16[4,128,256]{2,1,0:T(8,128)(2,1)S(1)}, u32[]{:S(2)}, u32[]{:S(2)}) collective-permute-start(bf16[4,128,256]{2,1,0:T(8,128)(2,1)} %collective-permute-done.1.rout), channel_id=1, source_target_pairs={{0,1},{1,0},{2,3},{3,2},{4,5},{5,4},{6,7},{7,6},{8,9},{9,8},{10,11... | collective-permute-start | bytes 786440 | tf_op jit(solution)/shard_map/ppermute | solution.py:21
  52.9 1.7 collective-permute-start.3
  52.9 1.6 collective-permute-start.4
  55.5 20.2 %copy-start.4 = (bf16[1024,128]{1,0:T(8,128)(2,1)S(1)}, bf16[1024,128]{1,0:T(8,128)(2,1)}, u32[]{:S(2)}) copy-start(bf16[1024,128]{1,0:T(8,128)(2,1)} %copy-done.3) | copy-start | bytes 786436
  58.4 9.0 %collective-permute-start.5 = (bf16[3,128,128]{2,1,0:T(8,128)(2,1)S(1)}, bf16[3,128,128]{2,1,0:T(8,128)(2,1)S(1)}, u32[]{:S(2)}, u32[]{:S(2)}) collective-permute-start(bf16[3,128,128]{2,1,0:T(8,128)(2,1)S(1)} %get-tuple-element.101), channel_id=1, source_target_pairs={{0,1},{1,0},{2,3},{3,2},{4,5},{5,4},{6,7},{7,6},{8,9},{9,8},{10,11... | collective-permute-start | bytes 294920 | tf_op jit(solution)/shard_map/ppermute | solution.py:21
  67.4 0.7 collective-permute-start.6
  68.1 7.6 %collective-permute-start.7 = (bf16[4,128,128]{2,1,0:T(8,128)(2,1)S(1)}, bf16[4,128,128]{2,1,0:T(8,128)(2,1)S(1)}, u32[]{:S(2)}, u32[]{:S(2)}) collective-permute-start(bf16[4,128,128]{2,1,0:T(8,128)(2,1)S(1)} %collective-permute-done.6.rout), channel_id=1, source_target_pairs={{0,1},{1,0},{2,3},{3,2},{4,5},{5,4},{6,7},{7,6},{8,9},{9,8},{10,11... | collective-permute-start | bytes 393224 | tf_op jit(solution)/shard_map/ppermute | solution.py:21
  77.5 1.5 collective-permute-start.8
  79.1 0.7 collective-permute-start.9
  79.8 12.0 %collective-permute-start.10 = (bf16[4,128,256]{2,1,0:T(8,128)(2,1)S(1)}, bf16[4,128,256]{2,1,0:T(8,128)(2,1)S(1)}, u32[]{:S(2)}, u32[]{:S(2)}) collective-permute-start(bf16[4,128,256]{2,1,0:T(8,128)(2,1)S(1)} %collective-permute-done.9.rout), channel_id=1, source_target_pairs={{0,1},{1,0},{2,3},{3,2},{4,5},{5,4},{6,7},{7,6},{8,9},{9,8},{10,11... | collective-permute-start | bytes 786440 | tf_op jit(solution)/shard_map/ppermute | solution.py:21
  94.1 1.4 collective-permute-start.11
  95.5 0.9 collective-permute-start.12
  96.3 7.7 %collective-permute-start.13 = (bf16[4,128,128]{2,1,0:T(8,128)(2,1)S(1)}, bf16[4,128,128]{2,1,0:T(8,128)(2,1)S(1)}, u32[]{:S(2)}, u32[]{:S(2)}) collective-permute-start(bf16[4,128,128]{2,1,0:T(8,128)(2,1)S(1)} %collective-permute-done.12.rout), channel_id=1, source_target_pairs={{0,1},{1,0},{2,3},{3,2},{4,5},{5,4},{6,7},{7,6},{8,9},{9,8},{10,11... | collective-permute-start | bytes 393224 | tf_op jit(solution)/shard_map/ppermute | solution.py:21
  105.9 1.5 collective-permute-start.14
  107.4 0.7 collective-permute-start.15
  108.1 11.8 %collective-permute-start.16 = (bf16[4,128,256]{2,1,0:T(8,128)(2,1)S(1)}, bf16[4,128,256]{2,1,0:T(8,128)(2,1)S(1)}, u32[]{:S(2)}, u32[]{:S(2)}) collective-permute-start(bf16[4,128,256]{2,1,0:T(8,128)(2,1)S(1)} %collective-permute-done.15.rout), channel_id=1, source_target_pairs={{0,1},{1,0},{2,3},{3,2},{4,5},{5,4},{6,7},{7,6},{8,9},{9,8},{10,11... | collective-permute-start | bytes 786440 | tf_op jit(solution)/shard_map/ppermute | solution.py:21
  122.2 1.4 collective-permute-start.17
  123.6 0.7 collective-permute-start.18
  124.3 7.7 %collective-permute-start.19 = (bf16[4,128,128]{2,1,0:T(8,128)(2,1)S(1)}, bf16[4,128,128]{2,1,0:T(8,128)(2,1)S(1)}, u32[]{:S(2)}, u32[]{:S(2)}) collective-permute-start(bf16[4,128,128]{2,1,0:T(8,128)(2,1)S(1)} %collective-permute-done.18.rout), channel_id=1, source_target_pairs={{0,1},{1,0},{2,3},{3,2},{4,5},{5,4},{6,7},{7,6},{8,9},{9,8},{10,11... | collective-permute-start | bytes 393224 | tf_op jit(solution)/shard_map/ppermute | solution.py:21
  136.1 1.4 collective-permute-start.20
  137.5 0.7 collective-permute-start.21
  138.2 8.3 %collective-permute-start.22 = (bf16[4,128,128]{2,1,0:T(8,128)(2,1)S(1)}, bf16[4,128,128]{2,1,0:T(8,128)(2,1)S(1)}, u32[]{:S(2)}, u32[]{:S(2)}) collective-permute-start(bf16[4,128,128]{2,1,0:T(8,128)(2,1)S(1)} %collective-permute-done.21.refs_3_), channel_id=1, source_target_pairs={{0,1},{1,0},{2,3},{3,2},{4,5},{5,4},{6,7},{7,6},{8,9},{9,8},{10,11... | collective-permute-start | bytes 393224 | tf_op jit(solution)/shard_map/ppermute | solution.py:21
  150.5 14.3 %copy-start.11 = (bf16[1024,128]{1,0:T(8,128)(2,1)S(1)}, bf16[1024,128]{1,0:T(8,128)(2,1)}, u32[]{:S(2)}) copy-start(bf16[1024,128]{1,0:T(8,128)(2,1)} %copy-done.10) | copy-start | bytes 786436
  150.5 1.6 collective-permute-start.23
  152.2 0.7 collective-permute-start.24
  152.9 12.0 %collective-permute-start.25 = (bf16[4,128,256]{2,1,0:T(8,128)(2,1)S(1)}, bf16[4,128,256]{2,1,0:T(8,128)(2,1)S(1)}, u32[]{:S(2)}, u32[]{:S(2)}) collective-permute-start(bf16[4,128,256]{2,1,0:T(8,128)(2,1)S(1)} %collective-permute-done.24.refs_15_), channel_id=1, source_target_pairs={{0,1},{1,0},{2,3},{3,2},{4,5},{5,4},{6,7},{7,6},{8,9},{9,8},{10,11... | collective-permute-start | bytes 786440 | tf_op jit(solution)/shard_map/ppermute | solution.py:21
  167.4 13.9 %copy-start.16 = (bf16[1024,128]{1,0:T(8,128)(2,1)}, bf16[1024,128]{1,0:T(8,128)(2,1)S(1)}, u32[]{:S(2)}) copy-start(bf16[1024,128]{1,0:T(8,128)(2,1)S(1)} %get-tuple-element.175.gx2) | copy-start | bytes 786436
  167.4 1.4 collective-permute-start.26
  168.9 0.9 collective-permute-start.27
  169.8 7.5 %collective-permute-start.28 = (bf16[4,128,128]{2,1,0:T(8,128)(2,1)S(1)}, bf16[4,128,128]{2,1,0:T(8,128)(2,1)S(1)}, u32[]{:S(2)}, u32[]{:S(2)}) collective-permute-start(bf16[4,128,128]{2,1,0:T(8,128)(2,1)S(1)} %collective-permute-done.27.refs_3_), channel_id=1, source_target_pairs={{0,1},{1,0},{2,3},{3,2},{4,5},{5,4},{6,7},{7,6},{8,9},{9,8},{10,11... | collective-permute-start | bytes 393224 | tf_op jit(solution)/shard_map/ppermute | solution.py:21
  181.3 14.3 %copy-start.9 = (bf16[1024,128]{1,0:T(8,128)(2,1)S(1)}, bf16[1024,128]{1,0:T(8,128)(2,1)}, u32[]{:S(2)}) copy-start(bf16[1024,128]{1,0:T(8,128)(2,1)} %copy-done.8) | copy-start | bytes 786436
  181.3 1.6 collective-permute-start.29
  182.9 0.7 collective-permute-start.30
  183.6 12.0 %collective-permute-start.31 = (bf16[4,128,256]{2,1,0:T(8,128)(2,1)S(1)}, bf16[4,128,256]{2,1,0:T(8,128)(2,1)S(1)}, u32[]{:S(2)}, u32[]{:S(2)}) collective-permute-start(bf16[4,128,256]{2,1,0:T(8,128)(2,1)S(1)} %collective-permute-done.30.refs_15_), channel_id=1, source_target_pairs={{0,1},{1,0},{2,3},{3,2},{4,5},{5,4},{6,7},{7,6},{8,9},{9,8},{10,11... | collective-permute-start | bytes 786440 | tf_op jit(solution)/shard_map/ppermute | solution.py:21
  198.1 14.0 %copy-start.18 = (bf16[1024,128]{1,0:T(8,128)(2,1)}, bf16[1024,128]{1,0:T(8,128)(2,1)S(1)}, u32[]{:S(2)}) copy-start(bf16[1024,128]{1,0:T(8,128)(2,1)S(1)} %get-tuple-element.174.gx1) | copy-start | bytes 786436
  198.1 1.4 collective-permute-start.32
  199.6 0.7 collective-permute-start.33
  200.3 7.7 %collective-permute-start.34 = (bf16[4,128,128]{2,1,0:T(8,128)(2,1)S(1)}, bf16[4,128,128]{2,1,0:T(8,128)(2,1)S(1)}, u32[]{:S(2)}, u32[]{:S(2)}) collective-permute-start(bf16[4,128,128]{2,1,0:T(8,128)(2,1)S(1)} %collective-permute-done.33.refs_3_), channel_id=1, source_target_pairs={{0,1},{1,0},{2,3},{3,2},{4,5},{5,4},{6,7},{7,6},{8,9},{9,8},{10,11... | collective-permute-start | bytes 393224 | tf_op jit(solution)/shard_map/ppermute | solution.py:21
  212.1 1.7 collective-permute-start.35
  213.9 0.7 collective-permute-start.36
  214.6 106.4 %collective-permute-start.37 = (bf16[4,128,256]{2,1,0:T(8,128)(2,1)S(1)}, bf16[4,128,256]{2,1,0:T(8,128)(2,1)S(1)}, u32[]{:S(2)}, u32[]{:S(2)}) collective-permute-start(bf16[4,128,256]{2,1,0:T(8,128)(2,1)S(1)} %collective-permute-done.36.rout), channel_id=1, source_target_pairs={{0,1},{1,0},{2,3},{3,2},{4,5},{5,4},{6,7},{7,6},{8,9},{9,8},{10,11... | collective-permute-start | bytes 786440 | tf_op jit(solution)/shard_map/ppermute | solution.py:21
  (19 other events, 39.3 us)
Sparse Core Ops, SparseCore 0:
  213.8 96.9 all-reduce.1

commit v2 on v1

v2 whole, which is shorter than its diff:
```python
import functools
import math

import jax
import jax.numpy as jnp
from jax import lax
from jax.experimental import pallas as pl
from jax.experimental.pallas import tpu as pltpu
from jax.sharding import PartitionSpec as P

BF = jnp.bfloat16
F32 = jnp.float32
T = 128
NT = 8
ROWS = NT * T
VMEM_LIMIT = 24 * 1024 * 1024


def swap(block, start):
    count = lax.axis_size("wide")
    return lax.ppermute(
        block, "wide", [p for i in range(start, count - 1, 2) for p in ((i, i + 1), (i + 1, i))]
    )


def swap_in(block):
    return swap(block, 0)


def swap_out(block):
    return swap(block, 1)


def exchange(pay_in, pay_out, far, middle):
    got_in = swap_in(pay_in)
    (ready,) = run(middle, "middle", (), (pay_out, got_in, far), [(pay_out.shape, BF)])
    got_out = swap_out(ready)
    return got_in, got_out, swap_in(got_out)


def dot(a, b):
    return jnp.dot(a, b, preferred_element_type=F32)


def dot_nt(a, b):
    return lax.dot_general(a, b, (((1,), (1,)), ((), ())), preferred_element_type=F32)


def dot_tn(a, b):
    return lax.dot_general(a, b, (((0,), (0,)), ((), ())), preferred_element_type=F32)


def tile(ref, i):
    start = i * T if isinstance(i, int) else pl.multiple_of(i * T, T)
    return ref.at[pl.ds(start, T)]


class Place:
    def __init__(self, meta):
        self.idx = lambda r, s: meta[4 * r + s]
        core = meta[32]
        self.core = core
        self.e_in = 7 - 7 * core
        self.n_in = 6 - 5 * core
        self.e_out = 7 * core
        self.n_out = 1 + 5 * core
        self.pos_in = 9 - 9 * core
        self.pos_out = 9 * core
        self.col_in = jnp.where(core == 0, meta[4 * 7 + 3], meta[3])
        self.col_out = jnp.where(core == 0, meta[3], meta[4 * 7 + 3])
        self.t_in = jnp.clip(self.col_in - 1, 0, NT - 1)
        self.t_out = jnp.clip(self.col_out - 1, 0, NT - 1)


def edge_kernel(meta, counts, first, last, e_in, e_out, et_in, et_out, f_out, ft_in, s_in, s_out):
    place = Place(meta)
    zero = place.core == 0
    for low, side_row, row_far, them, far in (
        (False, place.e_in, place.col_in, place.pos_in, place.pos_out),
        (True, place.e_out, place.col_out, place.pos_out, place.pos_in),
    ):
        top = zero if low else jnp.logical_not(zero)
        vals = [jnp.where(top, first[0, k].astype(F32), last[0, k].astype(F32)) for k in range(4)]
        inside = jnp.where(top, vals[2], vals[1])
        ahead = jnp.where(top, vals[1], vals[2])
        live = counts[side_row] > 3

        def third(flag):
            return vals[3] * jnp.where(jnp.logical_and(live, flag), 1.0, 0.0)

        is_them, is_far = row_far == them, row_far == far
        own = third(jnp.logical_not(jnp.logical_or(is_them, is_far)))
        e_ref, et_ref = (e_out, et_out) if low else (e_in, et_in)
        for k, v in enumerate((vals[0], inside, own)):
            e_ref[:, k * T : (k + 1) * T] = v.astype(BF)
            et_ref[k * T : (k + 1) * T] = v.T.astype(BF)
        s_ref = s_out if low else s_in
        s_ref[0] = ahead.astype(BF)
        s_ref[1] = third(is_them).astype(BF)
        if low:
            f_out[...] = third(is_far).astype(BF)
            s_in[3] = third(is_far).astype(BF)
        else:
            s_ref[2] = third(is_far).astype(BF)
            ft_in[...] = third(is_far).T.astype(BF)


def pick_rows(order, pick):
    lane = lax.broadcasted_iota(jnp.int32, (T, T), 1).astype(F32)
    for j in range(NT):
        wanted = jnp.broadcast_to(order[j : j + 1, :].astype(F32), (T, T)).T
        for k in range(NT):
            pick[j * T : (j + 1) * T, k * T : (k + 1) * T] = (
                (wanted == lane + float(k * T)).astype(F32).astype(BF)
            )


def split_f32(value, ref, start):
    for k in range(3):
        part = value.astype(BF)
        ref[:, start + k * T : start + (k + 1) * T] = part
        value = value - part.astype(F32)


def write_payload(place, own, e_in, e_out, pay_in, pay_out, lanes):
    for e_ref, pay, tiles in (
        (e_in, pay_in, (place.e_in, place.n_in, place.t_in)),
        (e_out, pay_out, (place.e_out, place.n_out, place.t_out)),
    ):
        picked = [tile(own, i)[...].astype(BF) for i in tiles]
        pay[0, :, lanes] = picked[0]
        pay[1, :, lanes] = dot(e_ref[...], jnp.concatenate(picked, axis=0)).astype(BF)


S_LANES, X_LANES = slice(0, T), slice(T, 2 * T)


def start_kernel(
    meta, order, inputs, state, e_in, e_out, x0, st, pay_in, pay_out, pick, parts
):
    place = Place(meta)
    pick_rows(order, pick)
    split_f32(state[...], parts, 0)
    parts[:, 3 * T :] = inputs[0]
    for h in range(4):
        rows = slice(h * 256, (h + 1) * 256)
        got = dot(pick[rows], parts[...])
        st[rows] = got[:, :T] + got[:, T : 2 * T] + got[:, 2 * T : 3 * T]
        x0[rows] = got[:, 3 * T :].astype(BF)
    write_payload(place, st, e_in, e_out, pay_in, pay_out, S_LANES)
    write_payload(place, x0, e_in, e_out, pay_in, pay_out, X_LANES)


def rest_kernel(order, in1, in2, cot, x1, x2, c0, c1, c2, pick, parts):
    pick_rows(order, pick)
    for k, src in enumerate((in1[0], in2[0], cot[0], cot[1], cot[2])):
        parts[:, k * T : (k + 1) * T] = src
    for h in range(4):
        rows = slice(h * 256, (h + 1) * 256)
        got = dot(pick[rows], parts[...]).astype(BF)
        for k, out in enumerate((x1, x2, c0, c1, c2)):
            out[rows] = got[:, k * T : (k + 1) * T]


def operator_kernel(counts, vals, vfg, vbg, vbd):
    for r in range(NT):
        live = jnp.where(counts[r] > 3, 1.0, 0.0)
        last = (vals[r, 3].astype(F32) * live).astype(BF)
        vfg[r, :, 0:T] = vals[r, 1]
        vfg[r, :, T : 2 * T] = vals[r, 0]
        vfg[r, :, 2 * T : 3 * T] = vals[r, 2]
        vfg[r, :, 3 * T :] = last
        vbg[r, :, T : 2 * T] = vals[r, 0].T
        if r > 0:
            vbg[r - 1, :, 2 * T :] = vals[r, 1].T
        else:
            vbd[8] = vals[r, 1].T
        if r < NT - 1:
            vbg[r + 1, :, 0:T] = vals[r, 2].T
        else:
            vbd[9] = vals[r, 2].T
        vbd[r] = last.T
    vbg[0, :, 0:T] = jnp.zeros((T, T), BF)
    vbg[NT - 1, :, 2 * T :] = jnp.zeros((T, T), BF)


def turn_kernel(vin, vout, tin, tout, tfar):
    for k in range(2):
        tin[:, k * T : (k + 1) * T] = vin[k].astype(F32).T.astype(BF)
        tout[:, k * T : (k + 1) * T] = vout[k].astype(F32).T.astype(BF)
    tfar[...] = vin[3].astype(F32).T.astype(BF)


def middle_forward(pay, got, far, out):
    out[0] = pay[0]
    out[1] = (pay[1].astype(F32) + dot(far[...], got[0])).astype(BF)


def middle_back(pay, got, far, out):
    out[0] = (pay[0].astype(F32) + dot(far[...], got[1])).astype(BF)
    out[1] = pay[1]


def forward_row(place, vfg, src, r):
    low = tile(src, place.idx(0, 1))[...] if r == 0 else tile(src, r)[...]
    high = tile(src, place.idx(7, 2))[...] if r == 7 else tile(src, r + 2)[...]
    picked = jnp.concatenate(
        [low, tile(src, r + 1)[...], high, tile(src, place.idx(r, 3))[...]], axis=0
    )
    return dot(vfg[r], picked)


def first_order(place, vfg, vin, vout, zext, d1, rin, rout, rfwd):
    tile(zext, place.pos_in)[...] = rin[0]
    tile(zext, place.pos_out)[...] = rout[0]
    for r in range(NT):
        tile(d1, r + 1)[...] = forward_row(place, vfg, zext, r).astype(BF)
    edge = tile(zext, place.e_in + 1)[...]
    lhs = jnp.concatenate([vin[0], vin[1], vin[2]], axis=1)
    total = rin[1].astype(F32) + dot(lhs, jnp.concatenate([edge, edge, rfwd[0]], axis=0))
    tile(d1, place.pos_in)[...] = total.astype(BF)
    edge = tile(zext, place.e_out + 1)[...]
    lhs = jnp.concatenate([vout[0], vout[1]], axis=1)
    total = rout[1].astype(F32) + dot(lhs, jnp.concatenate([edge, edge], axis=0))
    tile(d1, place.pos_out)[...] = total.astype(BF)


def second_order(place, vfg, zext, d1, r):
    z = tile(zext, r + 1)[...].astype(F32)
    return (2.0 * forward_row(place, vfg, d1, r) - z).astype(BF)


def gate_kernel(
    meta, st, x, rin, rout, rfwd, vfg, vin, vout, e_in, e_out, gw, gb, cw, cb,
    feats, r_out, u_out, q_out, xc_out, pay_in, pay_out, zext, d1,
):
    place = Place(meta)
    zext[T : T + ROWS, :T] = st[...].astype(BF)
    zext[T : T + ROWS, T:] = x[...]
    first_order(place, vfg, vin, vout, zext, d1, rin, rout, rfwd)
    for r in range(NT):
        d2 = second_order(place, vfg, zext, d1, r)
        z = tile(zext, r + 1)[...]
        one = tile(d1, r + 1)[...]
        row = jnp.concatenate(
            [z[:, T:], one[:, T:], d2[:, T:], z[:, :T], one[:, :T], d2[:, :T]], axis=1
        )
        tile(feats, r)[...] = row
    for h in range(4):
        rows = slice(h * 256, (h + 1) * 256)
        f = feats[rows]
        pre = dot(f, gw[...]) + gb[...]
        xc_out[rows] = dot(f[:, : 3 * T], cw[: 3 * T]) + cb[...]
        reset = jax.nn.sigmoid(pre[:, :T])
        r_out[rows] = reset
        u_out[rows] = jax.nn.sigmoid(pre[:, T:])
        q_out[rows] = (reset * st[rows]).astype(BF)
    write_payload(place, q_out, e_in, e_out, pay_in, pay_out, S_LANES)


def cand_kernel(meta, q, rin, rout, rfwd, vfg, vin, vout, e_in, e_out, cw, xc, u, st, *rest, last):
    if last:
        fq, c_out, zext, d1 = rest
    else:
        x_next, fq, c_out, st_out, pay_in, pay_out, zext, d1 = rest
    place = Place(meta)
    zext[T : T + ROWS] = q[...]
    first_order(place, vfg, vin, vout, zext, d1, rin, rout, rfwd)
    for r in range(NT):
        d2 = second_order(place, vfg, zext, d1, r)
        tile(fq, r)[...] = jnp.concatenate(
            [tile(zext, r + 1)[...], tile(d1, r + 1)[...], d2], axis=1
        )
    for h in range(4):
        rows = slice(h * 256, (h + 1) * 256)
        cand = jnp.tanh(dot(fq[rows], cw[3 * T :]) + xc[rows])
        c_out[rows] = cand
        if not last:
            st_out[rows] = u[rows] * st[rows] + (1.0 - u[rows]) * cand
    if not last:
        write_payload(place, st_out, e_in, e_out, pay_in, pay_out, S_LANES)
        write_payload(place, x_next, e_in, e_out, pay_in, pay_out, X_LANES)


def add_received(place, acc, rin, rout, rfwd, et_in, et_out, tfar):
    got_in = dot(et_in[...], rin[1])
    got_out = dot(et_out[...], rout[1])
    for i, block in (
        (place.e_in, got_in[:T] + rin[0].astype(F32) + dot(tfar[...], rfwd[1])),
        (place.n_in, got_in[T : 2 * T]),
        (place.t_in, got_in[2 * T :]),
        (place.e_out, got_out[:T] + rout[0].astype(F32)),
        (place.n_out, got_out[T : 2 * T]),
        (place.t_out, got_out[2 * T :]),
    ):
        tile(acc, i)[...] += block


def back_rows(place, vbg, vbd, y, acc, base):
    zero = jnp.zeros((T, acc.shape[1]), F32)
    tile(acc, 0)[...] = zero
    tile(acc, 9)[...] = zero
    for r in range(NT):
        lo, hi = max(r - 1, 0), min(r + 2, NT)
        lhs = vbg[r, :, (lo - r + 1) * T : (hi - r + 1) * T]
        tile(acc, r + 1)[...] = base(r, dot(lhs, y[lo * T : hi * T]))
    parts = [(place.idx(0, 1), 8, 0), (place.idx(7, 2), 9, 7)]
    parts += [(place.idx(r, 3), r, r) for r in range(NT)]
    for i, k, r in parts:
        tile(acc, i)[...] += dot(vbd[k], y[r * T : (r + 1) * T])


def diffuse_back(place, vbg, vbd, tin, tout, a, y, w, acc, pay_in, pay_out):
    for r in range(NT):
        rows = slice(r * T, (r + 1) * T)
        y[rows] = a(2, rows).astype(BF)
    back_rows(
        place, vbg, vbd, y, acc, lambda r, v: a(1, slice(r * T, (r + 1) * T)) * 0.5 + v
    )
    for e in range(NT + 2):
        tile(w, e)[...] = (2.0 * tile(acc, e)[...]).astype(BF)
    own = w.at[pl.ds(T, ROWS)]

    def second(r, v):
        rows = slice(r * T, (r + 1) * T)
        return a(0, rows) - a(2, rows) + v

    back_rows(place, vbg, vbd, own, acc, second)
    for pos, edge, vals, pay in (
        (place.pos_in, place.e_in, tin, pay_in),
        (place.pos_out, place.e_out, tout, pay_out),
    ):
        part = tile(w, pos)[...]
        tile(acc, edge + 1)[...] += dot(vals[...], jnp.concatenate([part, part], axis=0))
        pay[0] = tile(acc, pos)[...].astype(BF)
        pay[1] = part


def cand_back_kernel(*refs, first):
    refs = list(refs)
    take = lambda n: [refs.pop(0) for _ in range(n)]
    meta, cot, u, c, st, cw, vbg, vbd, tin, tout, et_in, et_out, tfar = take(13)
    if not first:
        gs_part, gx_part, rin, rout, rfwd = take(5)
    gp_out, ec_out, eu_out, gq_out, sums, pay_in, pay_out = take(7)
    if not first:
        (gx_out,) = take(1)
    gs, g, y, w, acc = take(5)
    place = Place(meta)
    if not first:
        gs[:, :T] = gs_part[...]
        gs[:, T:] = gx_part[...]
        add_received(place, gs, rin, rout, rfwd, et_in, et_out, tfar)
        gx_out[...] = gs[:, T:].astype(BF)
    sum_c = jnp.zeros((1, T), F32)
    sum_u = jnp.zeros((1, T), F32)
    for h in range(NT):
        rows = slice(h * T, (h + 1) * T)
        grad = cot[rows].astype(F32)
        if not first:
            grad = grad + gs[rows, :T]
        upd, cand = u[rows], c[rows]
        pre = grad * (1.0 - upd) * (1.0 - cand * cand)
        gate = grad * (st[rows] - cand) * upd * (1.0 - upd)
        gp_out[rows] = grad * upd
        ec_out[rows] = pre.astype(BF)
        eu_out[rows] = gate.astype(BF)
        sum_c = sum_c + jnp.sum(pre, axis=0, keepdims=True)
        sum_u = sum_u + jnp.sum(gate, axis=0, keepdims=True)
    sums[...] = jnp.broadcast_to(jnp.concatenate([sum_c, sum_u], axis=1), (8, 2 * T))
    g[...] = dot_nt(ec_out[...], cw[3 * T :])
    diffuse_back(
        place, vbg, vbd, tin, tout,
        lambda k, rows: g[rows, k * T : (k + 1) * T],
        y, w, acc, pay_in, pay_out,
    )
    gq_out[...] = acc[T : T + ROWS]


def gate_back_kernel(
    meta, gq_part, rin, rout, rfwd, gp, r_ref, st, ec, eu, gw, cw,
    vbg, vbd, tin, tout, et_in, et_out, tfar,
    gs_out, gx_out, er_out, sums, pay_in, pay_out, gq, eg, gps, g, y, w, acc,
):
    place = Place(meta)
    gq[...] = gq_part[...]
    add_received(place, gq, rin, rout, rfwd, et_in, et_out, tfar)
    sum_r = jnp.zeros((1, T), F32)
    for h in range(NT):
        rows = slice(h * T, (h + 1) * T)
        grad, reset = gq[rows], r_ref[rows]
        gps[rows] = gp[rows] + grad * reset
        pre = grad * st[rows] * reset * (1.0 - reset)
        eg[rows, :T] = pre.astype(BF)
        sum_r = sum_r + jnp.sum(pre, axis=0, keepdims=True)
    eg[:, T:] = eu[...]
    er_out[...] = eg[:, :T]
    sums[...] = jnp.broadcast_to(sum_r, (8, T))
    e = eg[...]
    for k in range(3):
        cols = slice(2 * k * T, (2 * k + 1) * T)
        g[:, cols] = dot_nt(e, gw[(3 + k) * T : (4 + k) * T])
        cols = slice((2 * k + 1) * T, (2 * k + 2) * T)
        g[:, cols] = dot_nt(e, gw[k * T : (k + 1) * T]) + dot_nt(
            ec[...], cw[k * T : (k + 1) * T]
        )
    diffuse_back(
        place, vbg, vbd, tin, tout,
        lambda k, rows: g[rows, 2 * k * T : 2 * (k + 1) * T],
        y, w, acc, pay_in, pay_out,
    )
    gs_out[...] = acc[T : T + ROWS, :T] + gps[...]
    gx_out[...] = acc[T : T + ROWS, T:]


def weight_cu_kernel(ec, eu, sums, feats, fq, *rest):
    out = rest[-1]
    x = feats[:, : 3 * T]
    out[:T, : 3 * T] = dot_tn(ec[...], x)
    out[:T, 3 * T :] = dot_tn(ec[...], fq[...])
    out[T : 2 * T] = dot_tn(eu[...], feats[...])
    row = jnp.concatenate([sums[...], jnp.zeros((8, 4 * T), F32)], axis=1)
    out[2 * T :] = jnp.concatenate([row, row], axis=0)
    if len(rest) > 1:
        out[...] += rest[0][...]


def weight_r_kernel(er, sums, feats, *rest):
    out = rest[-1]
    out[:T] = dot_tn(er[...], feats[...])
    row = jnp.concatenate([sums[...], jnp.zeros((8, 5 * T), F32)], axis=1)
    out[T:] = jnp.concatenate([row, row], axis=0)
    if len(rest) > 1:
        out[...] += rest[0][...]


def reduce_all(total, core):
    half = total.shape[1] // 2
    low, high = total[:, :half], total[:, half:]
    kept = jnp.where(core == 0, low, high)
    sent = jnp.where(core == 0, high, low).astype(BF)
    part = (kept + swap_in(sent).astype(F32)).astype(BF)
    count = lax.axis_size("wide")
    step = 2
    while step < count:
        other = lax.ppermute(part, "wide", [(i, i ^ step) for i in range(count)])
        part = (part.astype(F32) + other.astype(F32)).astype(BF)
        step *= 2
    return part, swap_in(part)


def weights_kernel(meta, cu_own, cu_other, r_own, r_other, gw, gb, cw, cb, *, scale):
    mine = meta[32] == 0

    def pick(own, other, side):
        a, b = own[...].astype(F32), other[...].astype(F32)
        return jnp.where(mine, a, b) if side == 0 else jnp.where(mine, b, a)

    for side in range(2):
        cu = pick(cu_own, cu_other, side) * scale
        r = pick(r_own, r_other, side) * scale
        for k in range(3):
            cols = slice(k * T, (k + 1) * T)
            rows = slice((3 * side + k) * T, (3 * side + k + 1) * T)
            cw[rows] = cu[:T, cols].T
            gw[rows, T:] = cu[T : 2 * T, cols].T
            gw[rows, :T] = r[:T, cols].T
        if side == 0:
            cb[...] = cu[2 * T : 2 * T + 1, :T]
            gb[:, T:] = cu[2 * T : 2 * T + 1, T : 2 * T]
            gb[:, :T] = r[T : T + 1, :T]


def finish_kernel(
    meta, order, gs_part, gx_part, rin, rout, rfwd, et_in, et_out, tfar, gx1, gx2,
    gi_out, gs_out, gs, parts,
):
    place = Place(meta)
    gs[:, :T] = gs_part[...]
    gs[:, T:] = gx_part[...]
    add_received(place, gs, rin, rout, rfwd, et_in, et_out, tfar)
    split_f32(gs[:, :T], parts, 0)
    parts[:, 3 * T : 4 * T] = gs[:, T:].astype(BF)
    parts[:, 4 * T : 5 * T] = gx1[...]
    parts[:, 5 * T :] = gx2[...]
    row = lax.broadcasted_iota(jnp.int32, (T, T), 0)
    for k in range(NT):
        put = jnp.concatenate(
            [
                (jnp.broadcast_to(order[j : j + 1, :], (T, T)) == row + k * T)
                .astype(F32)
                .astype(BF)
                for j in range(NT)
            ],
            axis=1,
        )
        rows = slice(k * T, (k + 1) * T)
        got = dot(put, parts[...])
        gs_out[rows] = got[:, :T] + got[:, T : 2 * T] + got[:, 2 * T : 3 * T]
        for t in range(3):
            gi_out[t, rows] = got[:, (3 + t) * T : (4 + t) * T].astype(BF)


SMEM = pl.BlockSpec(memory_space=pltpu.SMEM)
VMEM = pl.BlockSpec(memory_space=pltpu.VMEM)


def run(kernel, name, smem, args, outs, scratch=(), specs=None, flops=10**8):
    grid = (1,) if specs else ()
    specs = specs or [SMEM if i in smem else VMEM for i in range(len(args))]
    out_shape = [jax.ShapeDtypeStruct(s, d) for s, d in outs]
    moved = sum(x.size * x.dtype.itemsize for x in (*args, *out_shape))
    return pl.pallas_call(
        kernel,
        name=name,
        grid=grid,
        in_specs=specs,
        out_specs=[VMEM] * len(outs),
        out_shape=out_shape,
        scratch_shapes=[pltpu.VMEM(s, d) for s, d in scratch],
        cost_estimate=pl.CostEstimate(flops=flops, bytes_accessed=moved, transcendentals=0),
        compiler_params=pltpu.CompilerParams(vmem_limit_bytes=VMEM_LIMIT),
    )(*args)


def leading(block, at):
    zeros = (0,) * (len(block) - 1)
    return pl.BlockSpec(block, lambda i: (at,) + zeros, memory_space=pltpu.VMEM)


def per_device(
    inputs, state_init, cotangent, gate_w, gate_b, cand_w, cand_b,
    tile_vals, tile_cols, tile_counts, sector_order,
):
    device = lax.axis_index("wide")
    core = device % 2
    local_cols = tile_cols - (device * NT - 1)
    meta = jnp.concatenate([local_cols.reshape(-1), core[None]]).astype(jnp.int32)
    order = sector_order.reshape(NT, T)
    gb = gate_b.reshape(1, -1)
    cb = cand_b.reshape(1, -1)
    big = (ROWS, T)
    square = (T, T)
    flat, tall = ((T, 3 * T), BF), ((3 * T, T), BF)
    row_block, x_block = (1, 4, T, T), (1, ROWS, T)
    e_in, e_out, et_in, et_out, f_out, ft_in, s_in, s_out = run(
        edge_kernel, "edges", (), (meta, tile_counts, tile_vals, tile_vals),
        [flat, flat, tall, tall, (square, BF), (square, BF), ((4, T, T), BF), ((2, T, T), BF)],
        specs=[SMEM, SMEM, leading(row_block, 0), leading(row_block, NT - 1)],
    )
    vin, vout = swap_in(s_in), swap_out(s_out)
    x0, st, *pay = run(
        start_kernel, "start", (), (meta, order, inputs, state_init, e_in, e_out),
        [(big, BF), (big, F32)] + [((2, T, 2 * T), BF)] * 2,
        [((ROWS, ROWS), BF), ((ROWS, 4 * T), BF)],
        specs=[SMEM, VMEM, leading(x_block, 0), VMEM, VMEM, VMEM],
        flops=10**9,
    )
    vfg, vbg, vbd = run(
        operator_kernel, "operator", (0,), (tile_counts, tile_vals),
        [((NT, T, 4 * T), BF), ((NT, T, 3 * T), BF), ((NT + 2, T, T), BF)],
    )
    x1, x2, *cots = run(
        rest_kernel, "rest", (), (order, inputs, inputs, cotangent), [(big, BF)] * 5,
        [((ROWS, ROWS), BF), ((ROWS, 5 * T), BF)],
        specs=[VMEM, leading(x_block, 1), leading(x_block, 2), VMEM],
        flops=10**9,
    )
    tin, tout, tfar = run(
        turn_kernel, "turn", (), (vin, vout), [((T, 2 * T), BF)] * 2 + [(square, BF)]
    )
    xs = (x0, x1, x2)
    saved = []
    steps = inputs.shape[0]
    wide = ((NT + 2) * T, 2 * T)
    slim = ((NT + 2) * T, T)
    ops = (vfg, vin, vout, e_in, e_out)
    for t in range(steps):
        got = exchange(*pay, f_out, middle_forward)
        feats, r, u, q, xc, *pay = run(
            gate_kernel,
            "gate",
            (0,),
            (meta, st, xs[t], *got, *ops, gate_w, gb, cand_w, cb),
            [((ROWS, 6 * T), BF), (big, F32), (big, F32), (big, BF), (big, F32)]
            + [((2, T, T), BF)] * 2,
            [(wide, BF)] * 2,
        )
        got = exchange(*pay, f_out, middle_forward)
        last = t == steps - 1
        fq, c, *rest = run(
            functools.partial(cand_kernel, last=last),
            "cand",
            (0,),
            (meta, q, *got, *ops, cand_w, xc, u, st) + (() if last else (xs[t + 1],)),
            [((ROWS, 3 * T), BF), (big, F32)]
            + ([] if last else [(big, F32)] + [((2, T, 2 * T), BF)] * 2),
            [(slim, BF)] * 2,
        )
        saved.append((st, feats, r, u, fq, c))
        if not last:
            st, *pay = rest
    ops = (vbg, vbd, tin, tout, et_in, et_out, tfar)
    gxs = [None] * steps
    carry, cu_sum, r_sum = (), (), ()
    for t in reversed(range(steps)):
        st, feats, r, u, fq, c = saved[t]
        first = t == steps - 1
        gp, ec, eu, gq, sums, *rest = run(
            functools.partial(cand_back_kernel, first=first),
            "cand_back",
            (0,),
            (meta, cots[t], u, c, st, cand_w) + ops + carry,
            [(big, F32), (big, BF), (big, BF), (big, F32), ((8, 2 * T), F32)]
            + [((2, T, T), BF)] * 2
            + ([] if first else [(big, BF)]),
            [((ROWS, 2 * T), F32), ((ROWS, 3 * T), F32), (big, BF), (slim, BF), (slim, F32)],
        )
        if not first:
            gxs[t + 1] = rest[2]
        got = exchange(*rest[:2], ft_in, middle_back)
        cu_sum = run(
            weight_cu_kernel, "weight_cu", (), (ec, eu, sums, feats, fq, *cu_sum),
            [((2 * T + 16, 6 * T), F32)], flops=4 * 10**8,
        )
        gs_part, gx_part, er, sums, *rest = run(
            gate_back_kernel,
            "gate_back",
            (0,),
            (meta, gq, *got, gp, r, st, ec, eu, gate_w, cand_w) + ops,
            [(big, F32), (big, F32), (big, BF), ((8, T), F32)] + [((2, T, 2 * T), BF)] * 2,
            [
                (big, F32), ((ROWS, 2 * T), BF), (big, F32), ((ROWS, 6 * T), F32),
                ((ROWS, 2 * T), BF), (wide, BF), (wide, F32),
            ],
        )
        r_sum = run(
            weight_r_kernel, "weight_r", (), (er, sums, feats, *r_sum),
            [((T + 16, 6 * T), F32)], flops=2 * 10**8,
        )
        got = exchange(*rest, ft_in, middle_back)
        carry = (gs_part, gx_part, *got)
    cu = reduce_all(cu_sum[0], core)
    rr = reduce_all(r_sum[0], core)
    gi, gs = run(
        finish_kernel,
        "finish",
        (0,),
        (meta, order, *carry, et_in, et_out, tfar, gxs[1], gxs[2]),
        [((steps,) + big, BF), (big, F32)],
        [((ROWS, 2 * T), F32), ((ROWS, 6 * T), BF)],
    )
    scale = 1.0 / math.sqrt(ROWS * lax.axis_size("wide") * steps)
    gw, gb, cw, cb = run(
        functools.partial(weights_kernel, scale=scale),
        "weights",
        (0,),
        (meta, *cu, *rr),
        [((6 * T, 2 * T), F32), ((1, 2 * T), F32), ((6 * T, T), F32), ((1, T), F32)],
    )
    return gi, gs, gw, gb.reshape(-1), cw, cb.reshape(-1)


def solution(mesh):
    return jax.shard_map(
        per_device,
        mesh=mesh,
        in_specs=(
            P(None, ("parts", "wide"), None),
            P(("parts", "wide"), None),
            P(None, ("parts", "wide"), None),
            P(),
            P(),
            P(),
            P(),
            P(("parts", "wide"), None, None, None),
            P(("parts", "wide"), None),
            P(("parts", "wide")),
            P(("parts", "wide")),
        ),
        out_specs=(
            P(None, ("parts", "wide"), None),
            P(("parts", "wide"), None),
            P("parts", None),
            P("parts"),
            P("parts", None),
            P("parts"),
        ),
        check_vma=False,
    )
```

time: 333 us -> 205 us (0.62)
  waiting for transfers between devices: 105 us -> 35.8 us
  starting transfers between devices: 123 us -> 101 us
  between operations: 18.5 us -> 1.44 us
  other arithmetic: 18 us -> 1.19 us
  local copies, waits for them, and re-layouts: 24.7 us -> 17.6 us
  Pallas kernels: 42.8 us -> 47.4 us
    psum x1 -> x0, waiting for transfers between devices: 83.1 us -> none  [per_device(): grads = lax.psum(jnp.concatenate([wg[0], wc], axis=0), 'wide')]
    ppermute x38 -> x48, starting transfers between devices: 123 us -> 101 us  [the longest x42 88.2 us: swap(): lax.ppermute(block, 'wide', [p for i in range(start, count - 1, 2) for p...]
    ppermute x38 -> x48, waiting for transfers between devices: 21.9 us -> 35.8 us  [the longest x42 18.1 us: swap(): lax.ppermute(block, 'wide', [p for i in range(start, count - 1, 2) for p...]
    unnamed x6 -> x0, other arithmetic: 8.37 us -> none
    pallas_call x15 -> x37, Pallas kernels: 42.8 us -> 47.4 us  [run(): pl.pallas_call(kernel, name=name, grid=grid, in_specs=specs, out_specs=[V...]
    slice x15 -> x0, local copies, waits for them, and re-layouts: 3.84 us -> none  [the longest x2 1.68 us: edge_values(): col = lax.dynamic_index_in_dim(local_cols, row, 0, keepdims=False)[3]]
    concatenate x14 -> x0, other arithmetic: 3.59 us -> none  [the longest x6 1.74 us: exchange_forward(): got_out = swap_out(jnp.concatenate([pay_out, got_in[:1]], axis=0))]
    unnamed x59 -> x90, local copies, waits for them, and re-layouts: 15.8 us -> 17.4 us
  transfers between devices with their start and end apart: 39 -> 48, of which waited for: 23 -> 24; matrix products, arithmetic and copies ran while one was open for 8% -> 0% of each run, Pallas kernels for 0% -> 7%
where the time goes in v2:
time: 205 us
  starting transfers between devices  101 us (49%)
  Pallas kernels  47.4 us (23%)
  waiting for transfers between devices  35.8 us (17%)
  local copies, waits for them, and re-layouts  17.6 us (9%)
    ppermute x42, starting transfers between devices, swap(): lax.ppermute(block, 'wide', [p for i in range(start, count - 1, 2) for p...  88.2 us
    pallas_call x37, Pallas kernels, run(): pl.pallas_call(kernel, name=name, grid=grid, in_specs=specs, out_specs=[V...  47.4 us
    ppermute x42, waiting for transfers between devices, swap(): lax.ppermute(block, 'wide', [p for i in range(start, count - 1, 2) for p...  18.1 us
    ppermute x6, waiting for transfers between devices, reduce_all(): other = lax.ppermute(part, 'wide', [(i, i ^ step) for i in range(count)])  17.7 us
    unnamed x90, local copies, waits for them, and re-layouts  17.4 us
    ppermute x6, starting transfers between devices, reduce_all(): other = lax.ppermute(part, 'wide', [(i, i ^ step) for i in range(count)])  13.1 us
  transfers between devices with their start and end apart: 48, of which 24 were waited for; matrix products, arithmetic and copies ran while one was open for 0% of the time, Pallas kernels for 7%

profile of v2, /device:TPU:0, one launch (start us, length us, event | category | flops | bytes accessed | tf_op | source)
XLA Modules:
  0.0 204.7 jit_solution(12682573092178888925)
XLA Ops:
  1.6 1.2 copy-done.2
  4.8 2.3 %start.1 = (bf16[1024,128]{1,0:T(8,128)(2,1)S(1)}, f32[1024,128]{1,0:T(8,128)S(1)}, bf16[2,128,256]{2,1,0:T(8,128)(2,1)S(1)}, bf16[2,128,256]{2,1,0:T(8,128)(2,1)S(1)}) custom-call(s32[33]{0:T(128)S(1)} %pad_add_fusion.meta.refs_0_, s32[8,128]{1,0:T(8,128)S(1)} %bitcast.12, bf16[3,1024,128]{2,1,0:T(8,128)(2,1)S(1)} %copy-done.40, ...), custom_call_target="tpu_custom_call" | custom-call | flops 1000000000 | bytes 2560132 | tf_op jit(solution)/shard_map/start/pallas_call | solution.py:513
  7.6 1.0 collective-permute-done.got.rin
  9.4 4.3 %collective-permute-start.3 = (bf16[4,128,128]{2,1,0:T(8,128)(2,1)S(1)}, bf16[4,128,128]{2,1,0:T(8,128)(2,1)S(1)}, u32[]{:S(2)}, u32[]{:S(2)}) collective-permute-start(bf16[4,128,128]{2,1,0:T(8,128)(2,1)S(1)} %get-tuple-element.118), channel_id=1, source_target_pairs={{0,1},{1,0},{2,3},{3,2},{4,5},{5,4},{6,7},{7,6},{8,9},{9,8},{10,11... | collective-permute-start | bytes 393224 | tf_op jit(solution)/shard_map/ppermute | solution.py:21
  13.7 2.6 %collective-permute-start.2 = (bf16[2,128,256]{2,1,0:T(8,128)(2,1)S(1)}, bf16[2,128,256]{2,1,0:T(8,128)(2,1)S(1)}, u32[]{:S(2)}, u32[]{:S(2)}) collective-permute-start(bf16[2,128,256]{2,1,0:T(8,128)(2,1)S(1)} %collective-permute-done.1.rout), channel_id=1, source_target_pairs={{0,1},{1,0},{2,3},{3,2},{4,5},{5,4},{6,7},{7,6},{8,9},{9,8},{10,11... | collective-permute-start | bytes 393224 | tf_op jit(solution)/shard_map/ppermute | solution.py:21
  17.9 2.5 %gate.3 = (bf16[1024,768]{1,0:T(8,128)(2,1)S(1)}, f32[1024,128]{1,0:T(8,128)S(1)}, f32[1024,128]{1,0:T(8,128)S(1)}, bf16[1024,128]{1,0:T(8,128)(2,1)S(1)}, f32[1...) custom-call(s32[33]{0:T(128)S(1)} %pad_add_fusion.meta.refs_0_, ...), custom_call_target="tpu_custom_call" | custom-call | flops 100000000 | bytes 6751876 | tf_op jit(solution)/shard_map/gate/pallas_call | solution.py:513
  21.2 5.3 %collective-permute-start.5 = (bf16[2,128,128]{2,1,0:T(8,128)(2,1)S(1)}, bf16[2,128,128]{2,1,0:T(8,128)(2,1)S(1)}, u32[]{:S(2)}, u32[]{:S(2)}) collective-permute-start(bf16[2,128,128]{2,1,0:T(8,128)(2,1)S(1)} %get-tuple-element.122), channel_id=1, source_target_pairs={{0,1},{1,0},{2,3},{3,2},{4,5},{5,4},{6,7},{7,6},{8,9},{9,8},{10,11... | collective-permute-start | bytes 196616 | tf_op jit(solution)/shard_map/ppermute | solution.py:21
  28.3 6.3 %collective-permute-start.7 = (bf16[2,128,128]{2,1,0:T(8,128)(2,1)S(1)}, bf16[2,128,128]{2,1,0:T(8,128)(2,1)S(1)}, u32[]{:S(2)}, u32[]{:S(2)}) collective-permute-start(bf16[2,128,128]{2,1,0:T(8,128)(2,1)S(1)} %collective-permute-done.6.rout), channel_id=1, source_target_pairs={{0,1},{1,0},{2,3},{3,2},{4,5},{5,4},{6,7},{7,6},{8,9},{9,8},{10,11... | collective-permute-start | bytes 196616 | tf_op jit(solution)/shard_map/ppermute | solution.py:21
  34.6 2.1 %rest.1 = (bf16[1024,128]{1,0:T(8,128)(2,1)S(1)}, bf16[1024,128]{1,0:T(8,128)(2,1)S(1)}, bf16[1024,128]{1,0:T(8,128)(2,1)S(1)}, bf16[1024,128]{1,0:T(8,128)(2,1)S(1)}, bf16[1024,128]{1,0:T(8,128)(2,1)S(1)}) custom-call(s32[8,128]{1,0:T(8,128)S(1)} %bitcast.13, bf16[3,1024,128]{2,1,0:T(8,128)(2,1)S(1)} %copy-done.40, bf16[3,1024,128]{2,1,0:T(8,128)(2,1)S(1)} %copy-done.40, ...), custom_call_target="tpu_custom_call" | custom-call | flops 1000000000 | bytes 3674112 | tf_op jit(solution)/shard_map/rest/pallas_call | solution.py:513
  36.7 2.0 cand.3
  39.7 1.3 collective-permute-done.8.got.rin
  41.8 6.9 %collective-permute-start.10 = (bf16[2,128,256]{2,1,0:T(8,128)(2,1)S(1)}, bf16[2,128,256]{2,1,0:T(8,128)(2,1)S(1)}, u32[]{:S(2)}, u32[]{:S(2)}) collective-permute-start(bf16[2,128,256]{2,1,0:T(8,128)(2,1)S(1)} %collective-permute-done.9.rout), channel_id=1, source_target_pairs={{0,1},{1,0},{2,3},{3,2},{4,5},{5,4},{6,7},{7,6},{8,9},{9,8},{10,11... | collective-permute-start | bytes 393224 | tf_op jit(solution)/shard_map/ppermute | solution.py:21
  49.7 2.5 %gate.4 = (bf16[1024,768]{1,0:T(8,128)(2,1)S(1)}, f32[1024,128]{1,0:T(8,128)S(1)}, f32[1024,128]{1,0:T(8,128)S(1)}, bf16[1024,128]{1,0:T(8,128)(2,1)S(1)}, f32[1...) custom-call(s32[33]{0:T(128)S(1)} %pad_add_fusion.meta.refs_0_, ...), custom_call_target="tpu_custom_call" | custom-call | flops 100000000 | bytes 6751876 | tf_op jit(solution)/shard_map/gate/pallas_call | solution.py:513
  52.2 1.1 copy-done.8
  55.4 6.7 %collective-permute-start.13 = (bf16[2,128,128]{2,1,0:T(8,128)(2,1)S(1)}, bf16[2,128,128]{2,1,0:T(8,128)(2,1)S(1)}, u32[]{:S(2)}, u32[]{:S(2)}) collective-permute-start(bf16[2,128,128]{2,1,0:T(8,128)(2,1)S(1)} %collective-permute-done.12.rout), channel_id=1, source_target_pairs={{0,1},{1,0},{2,3},{3,2},{4,5},{5,4},{6,7},{7,6},{8,9},{9,8},{10,11... | collective-permute-start | bytes 196616 | tf_op jit(solution)/shard_map/ppermute | solution.py:21
  63.0 2.0 cand.4
  66.2 1.0 collective-permute-done.14.got.rin
  68.2 6.5 %collective-permute-start.16 = (bf16[2,128,256]{2,1,0:T(8,128)(2,1)S(1)}, bf16[2,128,256]{2,1,0:T(8,128)(2,1)S(1)}, u32[]{:S(2)}, u32[]{:S(2)}) collective-permute-start(bf16[2,128,256]{2,1,0:T(8,128)(2,1)S(1)} %collective-permute-done.15.rout), channel_id=1, source_target_pairs={{0,1},{1,0},{2,3},{3,2},{4,5},{5,4},{6,7},{7,6},{8,9},{9,8},{10,11... | collective-permute-start | bytes 393224 | tf_op jit(solution)/shard_map/ppermute | solution.py:21
  75.7 2.5 %gate.5 = (bf16[1024,768]{1,0:T(8,128)(2,1)S(1)}, f32[1024,128]{1,0:T(8,128)S(1)}, f32[1024,128]{1,0:T(8,128)S(1)}, bf16[1024,128]{1,0:T(8,128)(2,1)S(1)}, f32[1...) custom-call(s32[33]{0:T(128)S(1)} %pad_add_fusion.meta.refs_0_, ...), custom_call_target="tpu_custom_call" | custom-call | flops 100000000 | bytes 6751876 | tf_op jit(solution)/shard_map/gate/pallas_call | solution.py:513
  78.2 1.2 copy-done.4
  81.5 6.2 %collective-permute-start.19 = (bf16[2,128,128]{2,1,0:T(8,128)(2,1)S(1)}, bf16[2,128,128]{2,1,0:T(8,128)(2,1)S(1)}, u32[]{:S(2)}, u32[]{:S(2)}) collective-permute-start(bf16[2,128,128]{2,1,0:T(8,128)(2,1)S(1)} %collective-permute-done.18.rout), channel_id=1, source_target_pairs={{0,1},{1,0},{2,3},{3,2},{4,5},{5,4},{6,7},{7,6},{8,9},{9,8},{10,11... | collective-permute-start | bytes 196616 | tf_op jit(solution)/shard_map/ppermute | solution.py:21
  88.5 1.7 cand.5
  91.1 1.9 cand_back.3
  95.2 6.2 %collective-permute-start.22 = (bf16[2,128,128]{2,1,0:T(8,128)(2,1)S(1)}, bf16[2,128,128]{2,1,0:T(8,128)(2,1)S(1)}, u32[]{:S(2)}, u32[]{:S(2)}) collective-permute-start(bf16[2,128,128]{2,1,0:T(8,128)(2,1)S(1)} %collective-permute-done.21.rout), channel_id=1, source_target_pairs={{0,1},{1,0},{2,3},{3,2},{4,5},{5,4},{6,7},{7,6},{8,9},{9,8},{10,11... | collective-permute-start | bytes 196616 | tf_op jit(solution)/shard_map/ppermute | solution.py:21
  102.3 3.3 %gate_back.3 = (f32[1024,128]{1,0:T(8,128)S(1)}, f32[1024,128]{1,0:T(8,128)S(1)}, bf16[1024,128]{1,0:T(8,128)(2,1)S(1)}, f32[8,128]{1,0:T(8,128)S(1)}, bf16[2,12...) custom-call(s32[33]{0:T(128)S(1)} %pad_add_fusion.meta.refs_0_, f32[1024,128]{1,0:T(8,128)S(1)} %get-tuple-element.155.gq_part, ...), custom_call_target="tpu_custom_call" | custom-call | flops 100000000 | bytes 6459524 | tf_op jit(solution)/shard_map/gate_back/pallas_call | solution.py:513
  106.0 1.0 collective-permute-done.23.got.refs_15_
  107.9 6.8 %collective-permute-start.25 = (bf16[2,128,256]{2,1,0:T(8,128)(2,1)S(1)}, bf16[2,128,256]{2,1,0:T(8,128)(2,1)S(1)}, u32[]{:S(2)}, u32[]{:S(2)}) collective-permute-start(bf16[2,128,256]{2,1,0:T(8,128)(2,1)S(1)} %collective-permute-done.24.refs_16_), channel_id=1, source_target_pairs={{0,1},{1,0},{2,3},{3,2},{4,5},{5,4},{6,7},{7,6},{8,9},{9,8},{10,11... | collective-permute-start | bytes 393224 | tf_op jit(solution)/shard_map/ppermute | solution.py:21
  115.7 2.4 %cand_back.4 = (f32[1024,128]{1,0:T(8,128)S(1)}, bf16[1024,128]{1,0:T(8,128)(2,1)S(1)}, bf16[1024,128]{1,0:T(8,128)(2,1)S(1)}, f32[1024,128]{1,0:T(8,128)S(1)}, ...) custom-call(s32[33]{0:T(128)S(1)} %pad_add_fusion.meta.refs_0_, ...), custom_call_target="tpu_custom_call" | custom-call | flops 100000000 | bytes 6922372 | tf_op jit(solution)/shard_map/cand_back/pallas_call | solution.py:513
  120.4 5.9 %collective-permute-start.28 = (bf16[2,128,128]{2,1,0:T(8,128)(2,1)S(1)}, bf16[2,128,128]{2,1,0:T(8,128)(2,1)S(1)}, u32[]{:S(2)}, u32[]{:S(2)}) collective-permute-start(bf16[2,128,128]{2,1,0:T(8,128)(2,1)S(1)} %collective-permute-done.27.rout), channel_id=1, source_target_pairs={{0,1},{1,0},{2,3},{3,2},{4,5},{5,4},{6,7},{7,6},{8,9},{9,8},{10,11... | collective-permute-start | bytes 196616 | tf_op jit(solution)/shard_map/ppermute | solution.py:21
  127.3 3.3 %gate_back.4 = (f32[1024,128]{1,0:T(8,128)S(1)}, f32[1024,128]{1,0:T(8,128)S(1)}, bf16[1024,128]{1,0:T(8,128)(2,1)S(1)}, f32[8,128]{1,0:T(8,128)S(1)}, bf16[2,12...) custom-call(s32[33]{0:T(128)S(1)} %pad_add_fusion.meta.refs_0_, f32[1024,128]{1,0:T(8,128)S(1)} %get-tuple-element.167.gq_part, ...), custom_call_target="tpu_custom_call" | custom-call | flops 100000000 | bytes 6459524 | tf_op jit(solution)/shard_map/gate_back/pallas_call | solution.py:513
  131.7 1.0 collective-permute-done.29.got.refs_15_
  133.5 6.8 %collective-permute-start.31 = (bf16[2,128,256]{2,1,0:T(8,128)(2,1)S(1)}, bf16[2,128,256]{2,1,0:T(8,128)(2,1)S(1)}, u32[]{:S(2)}, u32[]{:S(2)}) collective-permute-start(bf16[2,128,256]{2,1,0:T(8,128)(2,1)S(1)} %collective-permute-done.30.refs_16_), channel_id=1, source_target_pairs={{0,1},{1,0},{2,3},{3,2},{4,5},{5,4},{6,7},{7,6},{8,9},{9,8},{10,11... | collective-permute-start | bytes 393224 | tf_op jit(solution)/shard_map/ppermute | solution.py:21
  141.4 2.9 %cand_back.5 = (f32[1024,128]{1,0:T(8,128)S(1)}, bf16[1024,128]{1,0:T(8,128)(2,1)S(1)}, bf16[1024,128]{1,0:T(8,128)(2,1)S(1)}, f32[1024,128]{1,0:T(8,128)S(1)}, ...) custom-call(s32[33]{0:T(128)S(1)} %pad_add_fusion.meta.refs_0_, ...), custom_call_target="tpu_custom_call" | custom-call | flops 100000000 | bytes 6922372 | tf_op jit(solution)/shard_map/cand_back/pallas_call | solution.py:513
  149.0 1.4 copy-done.5
  150.4 1.1 copy-done.17
  157.0 4.1 %collective-permute-start.34 = (bf16[2,128,128]{2,1,0:T(8,128)(2,1)S(1)}, bf16[2,128,128]{2,1,0:T(8,128)(2,1)S(1)}, u32[]{:S(2)}, u32[]{:S(2)}) collective-permute-start(bf16[2,128,128]{2,1,0:T(8,128)(2,1)S(1)} %collective-permute-done.33.rout), channel_id=1, source_target_pairs={{0,1},{1,0},{2,3},{3,2},{4,5},{5,4},{6,7},{7,6},{8,9},{9,8},{10,11... | collective-permute-start | bytes 196616 | tf_op jit(solution)/shard_map/ppermute | solution.py:21
  162.0 3.3 %gate_back.5 = (f32[1024,128]{1,0:T(8,128)S(1)}, f32[1024,128]{1,0:T(8,128)S(1)}, bf16[1024,128]{1,0:T(8,128)(2,1)S(1)}, f32[8,128]{1,0:T(8,128)S(1)}, bf16[2,12...) custom-call(s32[33]{0:T(128)S(1)} %pad_add_fusion.meta.refs_0_, f32[1024,128]{1,0:T(8,128)S(1)} %copy-done.27, ...), custom_call_target="tpu_custom_call" | custom-call | flops 100000000 | bytes 6459524 | tf_op jit(solution)/shard_map/gate_back/pallas_call | solution.py:513
  166.5 3.0 %collective-permute-start.39 = (bf16[272,384]{1,0:T(8,128)(2,1)S(1)}, bf16[272,384]{1,0:T(8,128)(2,1)S(1)}, u32[]{:S(2)}, u32[]{:S(2)}) collective-permute-start(bf16[272,384]{1,0:T(8,128)(2,1)S(1)} %add_convert_fusion.3), channel_id=1, source_target_pairs={{0,2},{1,3},{2,0},{3,1},{4,6},{5,7},{6,4},{7,5},{8,10},{9,11},{10,... | collective-permute-start | bytes 626696 | tf_op jit(solution)/shard_map/ppermute | solution.py:446
  171.4 4.1 %collective-permute-done.39 = bf16[272,384]{1,0:T(8,128)(2,1)S(1)} collective-permute-done((bf16[272,384]{1,0:T(8,128)(2,1)S(1)}, bf16[272,384]{1,0:T(8,128)(2,1)S(1)}, u32[]{:S(2)}, u32[]{:S(2)}) %collective-permute-start.39) | collective-permute-done | bytes 208928 | tf_op jit(solution)/shard_map/ppermute | solution.py:446
  175.6 2.4 %collective-permute-start.40 = (bf16[272,384]{1,0:T(8,128)(2,1)S(1)}, bf16[272,384]{1,0:T(8,128)(2,1)S(1)}, u32[]{:S(2)}, u32[]{:S(2)}) collective-permute-start(bf16[272,384]{1,0:T(8,128)(2,1)S(1)} %add_convert_fusion.2), channel_id=1, source_target_pairs={{0,4},{1,5},{2,6},{3,7},{4,0},{5,1},{6,2},{7,3},{8,12},{9,13},{10,... | collective-permute-start | bytes 626696 | tf_op jit(solution)/shard_map/ppermute | solution.py:446
  178.8 2.1 %collective-permute-start.45 = (bf16[144,384]{1,0:T(8,128)(2,1)S(1)}, bf16[144,384]{1,0:T(8,128)(2,1)S(1)}, u32[]{:S(2)}, u32[]{:S(2)}) collective-permute-start(bf16[144,384]{1,0:T(8,128)(2,1)S(1)} %add_convert_fusion.6), channel_id=1, source_target_pairs={{0,4},{1,5},{2,6},{3,7},{4,0},{5,1},{6,2},{7,3},{8,12},{9,13},{10,... | collective-permute-start | bytes 331784 | tf_op jit(solution)/shard_map/ppermute | solution.py:446
  180.9 2.3 %collective-permute-done.40 = bf16[272,384]{1,0:T(8,128)(2,1)S(1)} collective-permute-done((bf16[272,384]{1,0:T(8,128)(2,1)S(1)}, bf16[272,384]{1,0:T(8,128)(2,1)S(1)}, u32[]{:S(2)}, u32[]{:S(2)}) %collective-permute-start.40) | collective-permute-done | bytes 208928 | tf_op jit(solution)/shard_map/ppermute | solution.py:446
  183.3 2.5 %collective-permute-start.41 = (bf16[272,384]{1,0:T(8,128)(2,1)S(1)}, bf16[272,384]{1,0:T(8,128)(2,1)S(1)}, u32[]{:S(2)}, u32[]{:S(2)}) collective-permute-start(bf16[272,384]{1,0:T(8,128)(2,1)S(1)} %add_convert_fusion.1), channel_id=1, source_target_pairs={{0,8},{1,9},{2,10},{3,11},{4,12},{5,13},{6,14},{7,15},{8,0},{9,1},... | collective-permute-start | bytes 626696 | tf_op jit(solution)/shard_map/ppermute | solution.py:446
  185.9 2.3 %collective-permute-start.46 = (bf16[144,384]{1,0:T(8,128)(2,1)S(1)}, bf16[144,384]{1,0:T(8,128)(2,1)S(1)}, u32[]{:S(2)}, u32[]{:S(2)}) collective-permute-start(bf16[144,384]{1,0:T(8,128)(2,1)S(1)} %add_convert_fusion.5), channel_id=1, source_target_pairs={{0,8},{1,9},{2,10},{3,11},{4,12},{5,13},{6,14},{7,15},{8,0},{9,1},... | collective-permute-start | bytes 331784 | tf_op jit(solution)/shard_map/ppermute | solution.py:446
  188.2 9.4 %collective-permute-done.41 = bf16[272,384]{1,0:T(8,128)(2,1)S(1)} collective-permute-done((bf16[272,384]{1,0:T(8,128)(2,1)S(1)}, bf16[272,384]{1,0:T(8,128)(2,1)S(1)}, u32[]{:S(2)}, u32[]{:S(2)}) %collective-permute-start.41) | collective-permute-done | bytes 208928 | tf_op jit(solution)/shard_map/ppermute | solution.py:446
  197.7 1.0 collective-permute-done.46
  198.9 3.9 %finish.1 = (bf16[3,1024,128]{2,1,0:T(8,128)(2,1)}, f32[1024,128]{1,0:T(8,128)}) custom-call(s32[33]{0:T(128)S(1)} %pad_add_fusion.meta.refs_0_, s32[8,128]{1,0:T(8,128)S(1)} %bitcast.14, f32[1024,128]{1,0:T(8,128)S(1)} %get-tuple-element.185.gs_part, f32[1024,128]{1,0:T(8,128)S(1)} %get-tuple-element.186.gx_part, ...), custom_call_target="tpu_custom_call" | custom-call | flops 100000000 | bytes 3510404 | tf_op jit(solution)/shard_map/finish/pallas_call | solution.py:513
  202.8 1.9 weights.1
  (189 shorter events, 47.4 us)
Async XLA Ops:
  7.0 1.5 collective-permute-start
  8.7 5.0 %collective-permute-start.1 = (bf16[2,128,256]{2,1,0:T(8,128)(2,1)S(1)}, bf16[2,128,256]{2,1,0:T(8,128)(2,1)S(1)}, u32[]{:S(2)}, u32[]{:S(2)}) collective-permute-start(bf16[2,128,256]{2,1,0:T(8,128)(2,1)S(1)} %middle.12), channel_id=1, source_target_pairs={{1,2},{2,1},{3,4},{4,3},{5,6},{6,5},{7,8},{8,7},{9,10},{10,9},{11,... | collective-permute-start | bytes 393224 | tf_op jit(solution)/shard_map/ppermute | solution.py:21
  9.4 8.5 %collective-permute-start.3 = (bf16[4,128,128]{2,1,0:T(8,128)(2,1)S(1)}, bf16[4,128,128]{2,1,0:T(8,128)(2,1)S(1)}, u32[]{:S(2)}, u32[]{:S(2)}) collective-permute-start(bf16[4,128,128]{2,1,0:T(8,128)(2,1)S(1)} %get-tuple-element.118), channel_id=1, source_target_pairs={{0,1},{1,0},{2,3},{3,2},{4,5},{5,4},{6,7},{7,6},{8,9},{9,8},{10,11... | collective-permute-start | bytes 393224 | tf_op jit(solution)/shard_map/ppermute | solution.py:21
  13.7 4.2 %collective-permute-start.2 = (bf16[2,128,256]{2,1,0:T(8,128)(2,1)S(1)}, bf16[2,128,256]{2,1,0:T(8,128)(2,1)S(1)}, u32[]{:S(2)}, u32[]{:S(2)}) collective-permute-start(bf16[2,128,256]{2,1,0:T(8,128)(2,1)S(1)} %collective-permute-done.1.rout), channel_id=1, source_target_pairs={{0,1},{1,0},{2,3},{3,2},{4,5},{5,4},{6,7},{7,6},{8,9},{9,8},{10,11... | collective-permute-start | bytes 393224 | tf_op jit(solution)/shard_map/ppermute | solution.py:21
  16.2 1.6 collective-permute-start.4
  21.2 6.2 %collective-permute-start.5 = (bf16[2,128,128]{2,1,0:T(8,128)(2,1)S(1)}, bf16[2,128,128]{2,1,0:T(8,128)(2,1)S(1)}, u32[]{:S(2)}, u32[]{:S(2)}) collective-permute-start(bf16[2,128,128]{2,1,0:T(8,128)(2,1)S(1)} %get-tuple-element.122), channel_id=1, source_target_pairs={{0,1},{1,0},{2,3},{3,2},{4,5},{5,4},{6,7},{7,6},{8,9},{9,8},{10,11... | collective-permute-start | bytes 196616 | tf_op jit(solution)/shard_map/ppermute | solution.py:21
  27.6 0.7 collective-permute-start.6
  28.3 8.4 %collective-permute-start.7 = (bf16[2,128,128]{2,1,0:T(8,128)(2,1)S(1)}, bf16[2,128,128]{2,1,0:T(8,128)(2,1)S(1)}, u32[]{:S(2)}, u32[]{:S(2)}) collective-permute-start(bf16[2,128,128]{2,1,0:T(8,128)(2,1)S(1)} %collective-permute-done.6.rout), channel_id=1, source_target_pairs={{0,1},{1,0},{2,3},{3,2},{4,5},{5,4},{6,7},{7,6},{8,9},{9,8},{10,11... | collective-permute-start | bytes 196616 | tf_op jit(solution)/shard_map/ppermute | solution.py:21
  39.7 1.3 collective-permute-start.8
  41.2 0.7 collective-permute-start.9
  41.8 7.8 %collective-permute-start.10 = (bf16[2,128,256]{2,1,0:T(8,128)(2,1)S(1)}, bf16[2,128,256]{2,1,0:T(8,128)(2,1)S(1)}, u32[]{:S(2)}, u32[]{:S(2)}) collective-permute-start(bf16[2,128,256]{2,1,0:T(8,128)(2,1)S(1)} %collective-permute-done.9.rout), channel_id=1, source_target_pairs={{0,1},{1,0},{2,3},{3,2},{4,5},{5,4},{6,7},{7,6},{8,9},{9,8},{10,11... | collective-permute-start | bytes 393224 | tf_op jit(solution)/shard_map/ppermute | solution.py:21
  53.3 1.3 collective-permute-start.11
  54.7 0.7 collective-permute-start.12
  55.4 7.6 %collective-permute-start.13 = (bf16[2,128,128]{2,1,0:T(8,128)(2,1)S(1)}, bf16[2,128,128]{2,1,0:T(8,128)(2,1)S(1)}, u32[]{:S(2)}, u32[]{:S(2)}) collective-permute-start(bf16[2,128,128]{2,1,0:T(8,128)(2,1)S(1)} %collective-permute-done.12.rout), channel_id=1, source_target_pairs={{0,1},{1,0},{2,3},{3,2},{4,5},{5,4},{6,7},{7,6},{8,9},{9,8},{10,11... | collective-permute-start | bytes 196616 | tf_op jit(solution)/shard_map/ppermute | solution.py:21
  65.9 1.3 collective-permute-start.14
  67.4 0.9 collective-permute-start.15
  68.2 7.5 %collective-permute-start.16 = (bf16[2,128,256]{2,1,0:T(8,128)(2,1)S(1)}, bf16[2,128,256]{2,1,0:T(8,128)(2,1)S(1)}, u32[]{:S(2)}, u32[]{:S(2)}) collective-permute-start(bf16[2,128,256]{2,1,0:T(8,128)(2,1)S(1)} %collective-permute-done.15.rout), channel_id=1, source_target_pairs={{0,1},{1,0},{2,3},{3,2},{4,5},{5,4},{6,7},{7,6},{8,9},{9,8},{10,11... | collective-permute-start | bytes 393224 | tf_op jit(solution)/shard_map/ppermute | solution.py:21
  79.4 1.3 collective-permute-start.17
  80.8 0.7 collective-permute-start.18
  81.5 7.1 %collective-permute-start.19 = (bf16[2,128,128]{2,1,0:T(8,128)(2,1)S(1)}, bf16[2,128,128]{2,1,0:T(8,128)(2,1)S(1)}, u32[]{:S(2)}, u32[]{:S(2)}) collective-permute-start(bf16[2,128,128]{2,1,0:T(8,128)(2,1)S(1)} %collective-permute-done.18.rout), channel_id=1, source_target_pairs={{0,1},{1,0},{2,3},{3,2},{4,5},{5,4},{6,7},{7,6},{8,9},{9,8},{10,11... | collective-permute-start | bytes 196616 | tf_op jit(solution)/shard_map/ppermute | solution.py:21
  93.1 1.3 collective-permute-start.20
  94.5 0.7 collective-permute-start.21
  95.2 7.1 %collective-permute-start.22 = (bf16[2,128,128]{2,1,0:T(8,128)(2,1)S(1)}, bf16[2,128,128]{2,1,0:T(8,128)(2,1)S(1)}, u32[]{:S(2)}, u32[]{:S(2)}) collective-permute-start(bf16[2,128,128]{2,1,0:T(8,128)(2,1)S(1)} %collective-permute-done.21.rout), channel_id=1, source_target_pairs={{0,1},{1,0},{2,3},{3,2},{4,5},{5,4},{6,7},{7,6},{8,9},{9,8},{10,11... | collective-permute-start | bytes 196616 | tf_op jit(solution)/shard_map/ppermute | solution.py:21
  105.6 1.4 collective-permute-start.23
  107.2 0.7 collective-permute-start.24
  107.9 7.8 %collective-permute-start.25 = (bf16[2,128,256]{2,1,0:T(8,128)(2,1)S(1)}, bf16[2,128,256]{2,1,0:T(8,128)(2,1)S(1)}, u32[]{:S(2)}, u32[]{:S(2)}) collective-permute-start(bf16[2,128,256]{2,1,0:T(8,128)(2,1)S(1)} %collective-permute-done.24.refs_16_), channel_id=1, source_target_pairs={{0,1},{1,0},{2,3},{3,2},{4,5},{5,4},{6,7},{7,6},{8,9},{9,8},{10,11... | collective-permute-start | bytes 393224 | tf_op jit(solution)/shard_map/ppermute | solution.py:21
  118.1 1.3 collective-permute-start.26
  119.5 0.9 collective-permute-start.27
  120.4 6.8 %collective-permute-start.28 = (bf16[2,128,128]{2,1,0:T(8,128)(2,1)S(1)}, bf16[2,128,128]{2,1,0:T(8,128)(2,1)S(1)}, u32[]{:S(2)}, u32[]{:S(2)}) collective-permute-start(bf16[2,128,128]{2,1,0:T(8,128)(2,1)S(1)} %collective-permute-done.27.rout), channel_id=1, source_target_pairs={{0,1},{1,0},{2,3},{3,2},{4,5},{5,4},{6,7},{7,6},{8,9},{9,8},{10,11... | collective-permute-start | bytes 196616 | tf_op jit(solution)/shard_map/ppermute | solution.py:21
  131.3 1.3 collective-permute-start.29
  132.8 0.7 collective-permute-start.30
  133.5 7.8 %collective-permute-start.31 = (bf16[2,128,256]{2,1,0:T(8,128)(2,1)S(1)}, bf16[2,128,256]{2,1,0:T(8,128)(2,1)S(1)}, u32[]{:S(2)}, u32[]{:S(2)}) collective-permute-start(bf16[2,128,256]{2,1,0:T(8,128)(2,1)S(1)} %collective-permute-done.30.refs_16_), channel_id=1, source_target_pairs={{0,1},{1,0},{2,3},{3,2},{4,5},{5,4},{6,7},{7,6},{8,9},{9,8},{10,11... | collective-permute-start | bytes 393224 | tf_op jit(solution)/shard_map/ppermute | solution.py:21
  148.6 4.3 %collective-permute-start.32 = (bf16[2,128,128]{2,1,0:T(8,128)(2,1)}, bf16[2,128,128]{2,1,0:T(8,128)(2,1)S(1)}, u32[]{:S(2)}, u32[]{:S(2)}) collective-permute-start(bf16[2,128,128]{2,1,0:T(8,128)(2,1)} %get-tuple-element.179), channel_id=1, source_target_pairs={{0,1},{1,0},{2,3},{3,2},{4,5},{5,4},{6,7},{7,6},{8,9},{9,8},{10,11... | collective-permute-start | bytes 196616 | tf_op jit(solution)/shard_map/ppermute | solution.py:21
  153.1 3.9 %collective-permute-start.33 = (bf16[2,128,128]{2,1,0:T(8,128)(2,1)S(1)}, bf16[2,128,128]{2,1,0:T(8,128)(2,1)S(1)}, u32[]{:S(2)}, u32[]{:S(2)}) collective-permute-start(bf16[2,128,128]{2,1,0:T(8,128)(2,1)S(1)} %middle.22), channel_id=1, source_target_pairs={{1,2},{2,1},{3,4},{4,3},{5,6},{6,5},{7,8},{8,7},{9,10},{10,9},{11,... | collective-permute-start | bytes 196616 | tf_op jit(solution)/shard_map/ppermute | solution.py:21
  157.0 5.0 %collective-permute-start.34 = (bf16[2,128,128]{2,1,0:T(8,128)(2,1)S(1)}, bf16[2,128,128]{2,1,0:T(8,128)(2,1)S(1)}, u32[]{:S(2)}, u32[]{:S(2)}) collective-permute-start(bf16[2,128,128]{2,1,0:T(8,128)(2,1)S(1)} %collective-permute-done.33.rout), channel_id=1, source_target_pairs={{0,1},{1,0},{2,3},{3,2},{4,5},{5,4},{6,7},{7,6},{8,9},{9,8},{10,11... | collective-permute-start | bytes 196616 | tf_op jit(solution)/shard_map/ppermute | solution.py:21
  161.2 5.2 %collective-permute-start.38 = (bf16[272,384]{1,0:T(8,128)(2,1)S(1)}, bf16[272,384]{1,0:T(8,128)(2,1)S(1)}, u32[]{:S(2)}, u32[]{:S(2)}) collective-permute-start(bf16[272,384]{1,0:T(8,128)(2,1)S(1)} %select_convert_fusion), channel_id=1, source_target_pairs={{0,1},{1,0},{2,3},{3,2},{4,5},{5,4},{6,7},{7,6},{8,9},{9,8},{10,11... | collective-permute-start | bytes 626696 | tf_op jit(solution)/shard_map/ppermute | solution.py:21
  165.8 3.7 %collective-permute-start.43 = (bf16[144,384]{1,0:T(8,128)(2,1)S(1)}, bf16[144,384]{1,0:T(8,128)(2,1)S(1)}, u32[]{:S(2)}, u32[]{:S(2)}) collective-permute-start(bf16[144,384]{1,0:T(8,128)(2,1)S(1)} %select_convert_fusion.1), channel_id=1, source_target_pairs={{0,1},{1,0},{2,3},{3,2},{4,5},{5,4},{6,7},{7,6},{8,9},{9,8},{10,11... | collective-permute-start | bytes 331784 | tf_op jit(solution)/shard_map/ppermute | solution.py:21
  166.3 4.0 %collective-permute-start.35 = (bf16[2,128,256]{2,1,0:T(8,128)(2,1)S(1)}, bf16[2,128,256]{2,1,0:T(8,128)(2,1)S(1)}, u32[]{:S(2)}, u32[]{:S(2)}) collective-permute-start(bf16[2,128,256]{2,1,0:T(8,128)(2,1)S(1)} %get-tuple-element.187), channel_id=1, source_target_pairs={{0,1},{1,0},{2,3},{3,2},{4,5},{5,4},{6,7},{7,6},{8,9},{9,8},{10,11... | collective-permute-start | bytes 393224 | tf_op jit(solution)/shard_map/ppermute | solution.py:21
  166.5 9.0 %collective-permute-start.39 = (bf16[272,384]{1,0:T(8,128)(2,1)S(1)}, bf16[272,384]{1,0:T(8,128)(2,1)S(1)}, u32[]{:S(2)}, u32[]{:S(2)}) collective-permute-start(bf16[272,384]{1,0:T(8,128)(2,1)S(1)} %add_convert_fusion.3), channel_id=1, source_target_pairs={{0,2},{1,3},{2,0},{3,1},{4,6},{5,7},{6,4},{7,5},{8,10},{9,11},{10,... | collective-permute-start | bytes 626696 | tf_op jit(solution)/shard_map/ppermute | solution.py:446
  169.6 9.2 %collective-permute-start.44 = (bf16[144,384]{1,0:T(8,128)(2,1)S(1)}, bf16[144,384]{1,0:T(8,128)(2,1)S(1)}, u32[]{:S(2)}, u32[]{:S(2)}) collective-permute-start(bf16[144,384]{1,0:T(8,128)(2,1)S(1)} %add_convert_fusion.7), channel_id=1, source_target_pairs={{0,2},{1,3},{2,0},{3,1},{4,6},{5,7},{6,4},{7,5},{8,10},{9,11},{10,... | collective-permute-start | bytes 331784 | tf_op jit(solution)/shard_map/ppermute | solution.py:446
  170.4 10.5 %collective-permute-start.36 = (bf16[2,128,256]{2,1,0:T(8,128)(2,1)S(1)}, bf16[2,128,256]{2,1,0:T(8,128)(2,1)S(1)}, u32[]{:S(2)}, u32[]{:S(2)}) collective-permute-start(bf16[2,128,256]{2,1,0:T(8,128)(2,1)S(1)} %middle.23), channel_id=1, source_target_pairs={{1,2},{2,1},{3,4},{4,3},{5,6},{6,5},{7,8},{8,7},{9,10},{10,9},{11,... | collective-permute-start | bytes 393224 | tf_op jit(solution)/shard_map/ppermute | solution.py:21
  175.6 7.7 %collective-permute-start.40 = (bf16[272,384]{1,0:T(8,128)(2,1)S(1)}, bf16[272,384]{1,0:T(8,128)(2,1)S(1)}, u32[]{:S(2)}, u32[]{:S(2)}) collective-permute-start(bf16[272,384]{1,0:T(8,128)(2,1)S(1)} %add_convert_fusion.2), channel_id=1, source_target_pairs={{0,4},{1,5},{2,6},{3,7},{4,0},{5,1},{6,2},{7,3},{8,12},{9,13},{10,... | collective-permute-start | bytes 626696 | tf_op jit(solution)/shard_map/ppermute | solution.py:446
  178.8 7.0 %collective-permute-start.45 = (bf16[144,384]{1,0:T(8,128)(2,1)S(1)}, bf16[144,384]{1,0:T(8,128)(2,1)S(1)}, u32[]{:S(2)}, u32[]{:S(2)}) collective-permute-start(bf16[144,384]{1,0:T(8,128)(2,1)S(1)} %add_convert_fusion.6), channel_id=1, source_target_pairs={{0,4},{1,5},{2,6},{3,7},{4,0},{5,1},{6,2},{7,3},{8,12},{9,13},{10,... | collective-permute-start | bytes 331784 | tf_op jit(solution)/shard_map/ppermute | solution.py:446
  180.9 17.9 %collective-permute-start.37 = (bf16[2,128,256]{2,1,0:T(8,128)(2,1)S(1)}, bf16[2,128,256]{2,1,0:T(8,128)(2,1)S(1)}, u32[]{:S(2)}, u32[]{:S(2)}) collective-permute-start(bf16[2,128,256]{2,1,0:T(8,128)(2,1)S(1)} %collective-permute-done.36.rout), channel_id=1, source_target_pairs={{0,1},{1,0},{2,3},{3,2},{4,5},{5,4},{6,7},{7,6},{8,9},{9,8},{10,11... | collective-permute-start | bytes 393224 | tf_op jit(solution)/shard_map/ppermute | solution.py:21
  183.3 14.3 %collective-permute-start.41 = (bf16[272,384]{1,0:T(8,128)(2,1)S(1)}, bf16[272,384]{1,0:T(8,128)(2,1)S(1)}, u32[]{:S(2)}, u32[]{:S(2)}) collective-permute-start(bf16[272,384]{1,0:T(8,128)(2,1)S(1)} %add_convert_fusion.1), channel_id=1, source_target_pairs={{0,8},{1,9},{2,10},{3,11},{4,12},{5,13},{6,14},{7,15},{8,0},{9,1},... | collective-permute-start | bytes 626696 | tf_op jit(solution)/shard_map/ppermute | solution.py:446
  185.9 12.9 %collective-permute-start.46 = (bf16[144,384]{1,0:T(8,128)(2,1)S(1)}, bf16[144,384]{1,0:T(8,128)(2,1)S(1)}, u32[]{:S(2)}, u32[]{:S(2)}) collective-permute-start(bf16[144,384]{1,0:T(8,128)(2,1)S(1)} %add_convert_fusion.5), channel_id=1, source_target_pairs={{0,8},{1,9},{2,10},{3,11},{4,12},{5,13},{6,14},{7,15},{8,0},{9,1},... | collective-permute-start | bytes 331784 | tf_op jit(solution)/shard_map/ppermute | solution.py:446
  197.6 5.2 %collective-permute-start.42 = (bf16[272,384]{1,0:T(8,128)(2,1)S(1)}, bf16[272,384]{1,0:T(8,128)(2,1)S(1)}, u32[]{:S(2)}, u32[]{:S(2)}) collective-permute-start(bf16[272,384]{1,0:T(8,128)(2,1)S(1)} %add_convert_fusion.cu_own), channel_id=1, source_target_pairs={{0,1},{1,0},{2,3},{3,2},{4,5},{5,4},{6,7},{7,6},{8,9},{9,8},{10,11... | collective-permute-start | bytes 626696 | tf_op jit(solution)/shard_map/ppermute | solution.py:21
  198.8 4.0 %collective-permute-start.47 = (bf16[144,384]{1,0:T(8,128)(2,1)S(1)}, bf16[144,384]{1,0:T(8,128)(2,1)S(1)}, u32[]{:S(2)}, u32[]{:S(2)}) collective-permute-start(bf16[144,384]{1,0:T(8,128)(2,1)S(1)} %add_convert_fusion.4.r_own), channel_id=1, source_target_pairs={{0,1},{1,0},{2,3},{3,2},{4,5},{5,4},{6,7},{7,6},{8,9},{9,8},{10,11... | collective-permute-start | bytes 331784 | tf_op jit(solution)/shard_map/ppermute | solution.py:21
  (45 other events, 237.2 us)
